TPU v7x, 256 devices: a whole 4x4x8 slice. The times are simulated.
256 devices in a mesh: replica: 4 (over z_hi), fsdp: 64 (over z_lo, x, y, core).
Axes of the slice: x: 4, y: 4, z: 8 (z_hi: 4, z_lo: 2; z = z_hi * 2 + z_lo), core: 2. Of those that a mesh axis runs over, the one named last changes fastest.
Arguments:
- tokens: bfloat16 [16384, 6144], P(('replica', 'fsdp')), may hold values from -6 to 6
- expert_ids: int32 [16384, 2], P(('replica', 'fsdp')), may hold values from 0 to 7, as said below
- router_weight: bfloat16 [4, 8, 6144], P('replica'), may hold values from -6 to 6
- expert_weights: bfloat16 [4, 3, 6144, 8192], P('replica', None, None, 'fsdp'), may hold values from -6 to 6
- outer_params: float32 [768, 8192], P(None, 'fsdp'), may hold values from -6 to 6
- outer_momentum: float32 [768, 8192], P(None, 'fsdp'), may hold values from -3 to 3
- inner_drift: float32 [4, 768, 8192], P('replica', None, 'fsdp'), may hold values from -3 to 3
- frag_index: int32 [1], replicated, may hold values from 0 to 23
- out_grad: bfloat16 [16384, 6144], P(('replica', 'fsdp')), may hold values from -6 to 6
Outputs:
- expert_out: bfloat16 [16384, 6144], P(('replica', 'fsdp'))
- token_grad: bfloat16 [16384, 6144], P(('replica', 'fsdp'))
- new_params: float32 [768, 8192], P(None, 'fsdp')
- new_momentum: float32 [768, 8192], P(None, 'fsdp')
Inputs may be any that keep to these rules, and one draw needn't show every extreme that they name: `expert_ids`: each token names two different experts; in each aligned block of 64 tokens (the tokens of one device) exactly 3 tokens name expert 0.
All inputs are finite; a program needn't handle non-finite values.
Results may differ from a plain program's by a relative error of at most 0.0065.
Values may be sent and summed in bfloat16 or wider, within the bound.
A program may use at most 128 MiB of HBM per device.

v0:
```python
from functools import partial
import math

import jax
import jax.numpy as jnp
from jax import lax
from jax.sharding import PartitionSpec as P

FF = 8192
CAP = 3


inner_rate = 2.0
outer_rate = 0.7
momentum_decay = 0.9


def from_rows(left, right, factor, offset, length):
    part = lax.dynamic_slice_in_dim(left, offset, length, 1)
    return (
        lax.dot_general(part, right, (((0,), (0,)), ((), ())), preferred_element_type=jnp.float32)
        * factor
    )


def body(
    tokens,
    expert_ids,
    router_weight,
    expert_weights,
    outer_params,
    outer_momentum,
    inner_drift,
    frag_index,
    out_grad,
):
    width = tokens.shape[1]
    scale_in = 1.0 / math.sqrt(width)
    scale_hid = 1.0 / math.sqrt(FF)
    frag_rows = outer_params.shape[0]
    capacity = CAP
    contract = (((1,), (1,)), ((), ()))
    w_gate = expert_weights[0, 0]
    w_up = expert_weights[0, 1]
    w_down = expert_weights[0, 2]
    drift = inner_drift[0]
    replicas = lax.axis_size("replica")
    router_b = router_weight[0]
    router_f = router_b.astype(jnp.float32)
    experts = router_b.shape[0]
    routed = ((expert_ids[:, 0] == 0) | (expert_ids[:, 1] == 0)).astype(jnp.int32)
    other = expert_ids[:, 0] + expert_ids[:, 1]
    onehot = (other[:, None] == jnp.arange(experts, dtype=jnp.int32)[None, :]).astype(jnp.float32)
    logits = (
        lax.dot_general(tokens, router_b, contract, preferred_element_type=jnp.float32) * scale_in
    )
    logit_other = jnp.sum(logits * onehot, axis=1)
    prob = jax.nn.sigmoid(logits[:, 0] - logit_other)
    slots = jnp.cumsum(routed) - 1
    select = (
        (slots[None, :] == jnp.arange(capacity, dtype=jnp.int32)[:, None]) & (routed[None, :] == 1)
    ).astype(jnp.float32)
    select_b = select.astype(jnp.bfloat16)
    grad_tok = out_grad.astype(jnp.float32)
    back_grad = (prob[:, None] * grad_tok).astype(jnp.bfloat16)
    rows_in = jnp.dot(select_b, tokens, preferred_element_type=jnp.float32).astype(jnp.bfloat16)
    rows_grad = jnp.dot(select_b, back_grad, preferred_element_type=jnp.float32).astype(
        jnp.bfloat16
    )
    all_in, all_grad = (
        lax.all_gather(rows_in, "fsdp", axis=0, tiled=True),
        lax.all_gather(rows_grad, "fsdp", axis=0, tiled=True),
    )
    gate = jnp.dot(all_in, w_gate, preferred_element_type=jnp.float32) * scale_in
    up = jnp.dot(all_in, w_up, preferred_element_type=jnp.float32) * scale_in
    sigma = jax.nn.sigmoid(gate)
    active = gate * sigma
    hidden = (active * up).astype(jnp.bfloat16)
    d_hidden = jnp.dot(all_grad, w_down, preferred_element_type=jnp.float32) * scale_hid
    d_gate = (d_hidden * up * (sigma + gate * sigma * (1.0 - sigma))).astype(jnp.bfloat16)
    d_up = (d_hidden * active).astype(jnp.bfloat16)
    rows_out = lax.psum_scatter(
        lax.dot_general(hidden, w_down, contract, preferred_element_type=jnp.float32) * scale_hid,
        "fsdp",
        scatter_dimension=0,
        tiled=True,
    )
    rows_dx = lax.psum_scatter(
        (
            lax.dot_general(d_gate, w_gate, contract, preferred_element_type=jnp.float32)
            + lax.dot_general(d_up, w_up, contract, preferred_element_type=jnp.float32)
        )
        * scale_in,
        "fsdp",
        scatter_dimension=0,
        tiled=True,
    )
    expert_tok = jnp.dot(select.T, rows_out, precision=lax.Precision.HIGHEST)
    mixed = (prob[:, None] * expert_tok).astype(jnp.bfloat16)
    d_prob = jnp.sum(grad_tok * expert_tok, axis=1)
    d_logit = d_prob * prob * (1.0 - prob)
    dx_tok = jnp.dot(select.T, rows_dx, precision=lax.Precision.HIGHEST)
    router_other = jnp.dot(onehot, router_f, precision=lax.Precision.HIGHEST)
    differ = router_f[0][None, :] - router_other
    token_grad = (dx_tok + (d_logit * scale_in)[:, None] * differ).astype(jnp.bfloat16)
    frag = frag_index[0]
    per_mat = width // frag_rows
    matrix = frag // per_mat
    offset = frag % per_mat * frag_rows
    frag_grad = lax.switch(
        matrix,
        [
            partial(from_rows, all_in, d_gate, scale_in, offset, frag_rows),
            partial(from_rows, all_in, d_up, scale_in, offset, frag_rows),
            partial(from_rows, all_grad, hidden, scale_hid, offset, frag_rows),
        ],
    )
    step_part = inner_rate * frag_grad
    total = lax.psum(step_part - drift, "replica")
    pseudo = total / replicas
    new_momentum = momentum_decay * outer_momentum + pseudo
    new_params = outer_params - outer_rate * (pseudo + momentum_decay * new_momentum)
    return (mixed, token_grad, new_params, new_momentum)


def solution(mesh):
    in_specs = (
        P(("replica", "fsdp"), None),
        P(("replica", "fsdp"), None),
        P("replica", None, None),
        P("replica", None, None, "fsdp"),
        P(None, "fsdp"),
        P(None, "fsdp"),
        P("replica", None, "fsdp"),
        P(),
        P(("replica", "fsdp"), None),
    )
    out_specs = (
        P(("replica", "fsdp"), None),
        P(("replica", "fsdp"), None),
        P(None, "fsdp"),
        P(None, "fsdp"),
    )
    return jax.shard_map(body, mesh=mesh, in_specs=in_specs, out_specs=out_specs, check_vma=False)
```

profile of v0, /device:TPU:6, one launch (start us, length us, event | category | flops | bytes accessed | tf_op | source)
XLA Modules:
  0.0 879.2 jit_solution(5808895623004833200)
XLA Ops:
  7.2 0.8 compare_bitcast_fusion
  8.0 0.1 copy.15
  8.1 0.1 reduce-window.8
  8.2 0.1 add_reduce_fusion
  8.3 0.8 fusion.10
  9.2 0.0 all-gather.7.cloned.1.call-start
  9.2 0.8 add_bitcast_fusion
  10.0 1.2 select_reduce_fusion
  11.2 2.1 fusion.11
  13.3 0.0 all-reduce.6.cloned.1.call-start
  14.1 105.5 %all-gather.5.cloned.1.call-done = bf16[64,3,6144]{2,1,0:T(4,128)(2,1)} async-done(((bf16[1,3,6144]{2,1,0:T(4,128)(2,1)}), bf16[64,3,6144]{2,1,0:T(4,128)(2,1)}) %all-gather.5.cloned.1.call-update) | async-done | bytes 2359312 | tf_op jit(solution)/shard_map/all_gather | solution.py:71
  119.6 5.4 reshape.59
  124.9 2.2 fusion.30
  127.1 2.2 fusion.33
  129.3 98.9 %all-gather.7.cloned.1.call-done = bf16[64,3,6144]{2,1,0:T(4,128)(2,1)} async-done(((bf16[1,3,6144]{2,1,0:T(4,128)(2,1)}), bf16[64,3,6144]{2,1,0:T(4,128)(2,1)}) %all-gather.7.cloned.1.call-update) | async-done | bytes 2359312 | tf_op jit(solution)/shard_map/all_gather | solution.py:72
  228.2 6.8 reshape.61
  235.0 3.5 multiply_convert_fusion.1
  238.5 4.3 fusion.20
  242.8 1.3 conditional.1
  242.8 1.3 convolution_multiply_fusion.1
  244.1 1.8 bitcast_subtract_fusion
  245.9 0.0 all-reduce.8.cloned.1.call-start
  245.9 5.7 fusion.6
  251.7 4.4 convolution_multiply_fusion.3
  256.1 0.6 copy-done.7
  256.8 0.6 dynamic-slice
  258.0 40.2 %all-reduce.6.cloned.1.call-done = f32[768,128]{1,0:T(8,128)} async-done(((f32[768,128]{1,0:T(8,128)}), f32[768,128]{1,0:T(8,128)}) %all-reduce.6.cloned.1.call-update) | async-done | bytes 393232 | tf_op jit(solution)/shard_map/psum | solution.py:119
  298.2 2.0 multiply_subtract_fusion
  300.2 566.5 %all-reduce.8.cloned.1.call-done = (f32[192,6144]{1,0:T(8,128)}, f32[192,6144]{1,0:T(8,128)}) async-done(((f32[192,6144]{1,0:T(8,128)}, f32[192,6144]{1,0:T(8,128)}), (f32[192,6144]{1,0:T(8,128)}, f32[192,6144]{1,0:T(8,128)})) %all-reduce.8.cloned.1.call-update) | async-done | bytes 9437200
  866.7 2.9 fusion.13
  869.6 1.8 fusion.41
  871.4 1.3 fusion.9
  (22 shorter events, 0.2 us)
Async XLA Ops:
  7.2 1.2 copy-start
  7.2 112.4 %all-gather.5.cloned.1.call-start = ((), (), s32[]{:S(2)}) async-start(), calls=%async_computation.1 | async-start | bytes 3194880 | tf_op jit(solution)/shard_map/all_gather | solution.py:71
  9.2 219.0 %all-gather.7.cloned.1.call-start = ((), (), s32[]{:S(2)}) async-start(), calls=%async_computation.2 | async-start | bytes 3194880 | tf_op jit(solution)/shard_map/all_gather | solution.py:72
  13.3 284.9 %all-reduce.6.cloned.1.call-start = ((), (), s32[]{:S(2)}) async-start(), calls=%async_computation | async-start | bytes 786432 | tf_op jit(solution)/shard_map/psum | solution.py:119
  245.9 5.8 copy-start.5
  245.9 620.7 %all-reduce.8.cloned.1.call-start = ((), (), s32[]{:S(2)}) async-start(), calls=%async_computation.3 | async-start | bytes 18874368
  256.1 0.7 copy-start.7
  256.1 1.9 copy-start.2
  256.1 42.1 %copy-start.3 = (f32[768,128]{1,0:T(8,128)S(1)}, f32[768,128]{1,0:T(8,128)}, u32[]{:S(2)}) copy-start(f32[768,128]{1,0:T(8,128)} %param.16) | copy-start | bytes 1179652
  256.1 42.1 %copy-start.4 = (f32[768,128]{1,0:T(8,128)S(1)}, f32[768,128]{1,0:T(8,128)}, u32[]{:S(2)}) copy-start(f32[768,128]{1,0:T(8,128)} %param.17) | copy-start | bytes 1179652
  256.1 610.6 %copy-start.1 = (bf16[64,6144]{1,0:T(8,128)(2,1)S(1)}, bf16[64,6144]{1,0:T(8,128)(2,1)}, u32[]{:S(2)}) copy-start(bf16[64,6144]{1,0:T(8,128)(2,1)} %param.20) | copy-start | bytes 2359300
Sparse Core Ops, SparseCore 0:
  10.4 109.0 all-gather.4
  122.0 106.1 all-gather.6
  246.0 52.1 all-reduce.5
  300.9 565.6 all-reduce.7
where the time goes:
time: 895 us; the launch traced here: 879 us
  waiting for transfers between devices  811 us (91%)
  matrix products  33.7 us (4%)
  between operations  15.2 us (2%)
  local copies, waits for them, and re-layouts  13.5 us (2%)
    unnamed x5, waiting for transfers between devices  567 us
    all_gather x1, waiting for transfers between devices, body(): lax.all_gather(rows_in, 'fsdp', axis=0, tiled=True)  105 us
    all_gather x1, waiting for transfers between devices, body(): lax.all_gather(rows_grad, 'fsdp', axis=0, tiled=True)  98.9 us
    psum x1, waiting for transfers between devices, body(): total = lax.psum(step_part - drift, 'replica')  40.2 us
  transfers between devices with their start and end apart: 4, of which 4 were waited for; matrix products, arithmetic and copies ran while one was open for 3% of the time, Pallas kernels for 0%

commit v1 on v0

v1 whole, which is shorter than its diff:
```python
import math

import jax
import jax.numpy as jnp
from jax import lax
from jax.experimental import pallas as pl
from jax.experimental.pallas import tpu as pltpu
from jax.sharding import PartitionSpec as P

D = 6144
FF = 8192
EXPERTS = 8
CAP = 3
FR = 768
TOK = 64
KC = 16
LC = D // KC
BR = CAP * KC
NX = 4
NY = 4
NZ = 2
HID = 128
PLANE_TOK = 96
ROWS = 192
QR = FR // 4

inner_rate = 2.0
outer_rate = 0.7
momentum_decay = 0.9
scale_in = 1.0 / math.sqrt(D)
scale_hid = 1.0 / math.sqrt(FF)

MESH = pl.DeviceIdType.MESH
F32 = jnp.float32
BF16 = jnp.bfloat16
NT = (((1,), (1,)), ((), ()))
TN = (((0,), (0,)), ((), ()))


def dot(a, b, dims=(((1,), (0,)), ((), ()))):
    return lax.dot_general(a, b, dims, preferred_element_type=F32)


def iota(shape, dim):
    return lax.broadcasted_iota(jnp.int32, shape, dim)


def one(mask):
    return jnp.where(mask, 1.0, 0.0)


def row(slab, z, p):
    return ((slab * NZ + z) * 4 + p) * BR


def id_rows(ids):
    id0, id1 = ids[0:1, :], ids[1:2, :]
    at = iota((16, TOK), 0)
    routed = one((id0 == 0) | (id1 == 0))
    other = (id0 + id1).astype(F32)
    return jnp.where(at == 0, routed, jnp.where(at == 1, other, 0.0)).astype(BF16)


def kernel(
    tokens,
    ids,
    router,
    weights,
    drift,
    frag,
    grads,
    out_rows,
    out_pseudo,
    tokv,
    grdv,
    wgu,
    wdn,
    drfv,
    perm,
    ag,
    xv,
    gv,
    yv,
    rb,
    sb,
    t2,
    d2,
    t1,
    d1,
    zr,
    fq,
    fb,
    fr,
    ps,
    load_sem,
    ag_recv,
    z_send,
    r1_send,
    r2_send,
    sib_send,
    rs_sib_send,
    rs_sib_recv,
    t2_send,
    t2_recv,
    d2_send,
    d2_recv,
    t1_send,
    t1_recv,
    d1_send,
    d1_recv,
    zr_send,
    zr_recv,
    q_send,
    q_recv,
    p_send,
    p_recv,
):
    rep = lax.axis_index("replica")
    me = lax.axis_index("fsdp")
    core = me % 2
    py = (me // 2) % NY
    px = (me // (2 * NY)) % NX
    pz = me // (2 * NY * NX)
    first = 1 - core

    def dev(z, x, y, c):
        return {"fsdp": ((z * NX + x) * NY + y) * 2 + c}

    def ring_x(step):
        return dev(pz, (px + step) % NX, py, core)

    def ring_y(step):
        return dev(pz, px, (py + step) % NY, core)

    def pick(a, b):
        return {"fsdp": first * a["fsdp"] + core * b["fsdp"]}

    up1, dn1 = pick(ring_x(1), ring_y(1)), pick(ring_x(3), ring_y(3))
    up2, dn2 = pick(ring_y(1), ring_x(1)), pick(ring_y(3), ring_x(3))
    zpart = dev(1 - pz, px, py, core)
    sib = dev(pz, px, py, 1 - core)
    reps = [{"replica": (rep + d) % 4} for d in (1, 2, 3)]

    def load(src, dst, i):
        c = pltpu.make_async_copy(src, dst, load_sem.at[i])
        c.start()
        return c

    load_tok = load(tokens, tokv, 0)
    load_grd = load(grads, grdv, 1)

    barrier = pltpu.get_barrier_semaphore()
    peers = [up1, dn1, up2, dn2, zpart, sib] + reps
    for p in peers:
        pl.semaphore_signal(barrier, inc=1, device_id=p, device_id_type=MESH)

    load_g = load(weights.at[0, 0], wgu.at[:, 0:HID], 2)
    load_u = load(weights.at[0, 1], wgu.at[:, HID : 2 * HID], 3)
    load_d = load(weights.at[0, 2], wdn, 4)
    load_f = load(drift.at[0], drfv, 5)

    def send(src, dst, ssem, rsem, to):
        c = pltpu.make_async_remote_copy(
            src_ref=src, dst_ref=dst, send_sem=ssem, recv_sem=rsem,
            device_id=to, device_id_type=MESH,
        )
        c.start()
        return c

    def arrived(dst, rsem):
        pltpu.make_async_copy(dst, dst, rsem).wait()

    pending = []

    rows8 = id_rows(ids)
    wide = (TOK, KC * TOK)
    tiled = dot(rows8, one(iota(wide, 0) == iota(wide, 1) % TOK).astype(BF16))
    count = dot(rows8, one(iota(wide, 0) <= iota(wide, 1) % TOK).astype(BF16))
    sshape = (BR, KC * TOK)
    smask = (
        (tiled[0:1] > 0.5)
        & (count[0:1] - 1.0 == (iota(sshape, 0) // KC).astype(F32))
        & (iota(sshape, 0) % KC == iota(sshape, 1) // TOK)
    )
    select = one(smask).astype(BF16)
    other48 = jnp.sum(jnp.where(smask, tiled[1:2], 0.0), axis=1, keepdims=True)
    dshape = (BR, KC * EXPERTS)
    expert = iota(dshape, 1) % EXPERTS
    signs = jnp.where(
        iota(dshape, 0) % KC == iota(dshape, 1) // EXPERTS,
        one(expert == 0) - one(expert.astype(F32) == other48),
        0.0,
    ).astype(BF16)
    rw = router[0].astype(F32)
    router2 = jnp.concatenate([rw[:, k * LC : (k + 1) * LC] for k in range(KC)], axis=0)
    differ = dot(signs, router2.astype(BF16))

    pshape = (256, 256)
    perm[...] = one(
        (iota(pshape, 0) // 16 == iota(pshape, 1) % 16)
        & (iota(pshape, 0) % 16 == iota(pshape, 1) // 16)
    ).astype(BF16)

    def fold(ref):
        stacked = jnp.concatenate([ref[:, k * LC : (k + 1) * LC] for k in range(KC)], axis=0)
        return dot(select, stacked)

    load_tok.wait()
    xsel = fold(tokv)
    ag[0, 0, 0:BR, :] = xsel.astype(BF16)
    logit = jnp.sum((xsel * differ).reshape(CAP, KC, LC), axis=(1, 2), keepdims=True)
    prob = jax.nn.sigmoid(jnp.broadcast_to(logit * scale_in, (CAP, KC, LC)).reshape(BR, LC))
    load_grd.wait()
    gsel = fold(grdv)
    ag[1, 0, 0:BR, :] = (prob * gsel).astype(BF16)

    pl.semaphore_wait(barrier, len(peers))

    def piece(plane, slab, z, p):
        return ag.at[:, plane, pl.ds(row(slab, z, p), BR), :]

    def ag_sem(plane, slab, z, p):
        return ag_recv.at[((plane * 4 + slab) * 2 + z) * 4 + p]

    def push(src_key, dst_key, ssem, to):
        pending.append(send(piece(*src_key), piece(*dst_key), ssem, ag_sem(*dst_key), to))

    def to_sib(slab, z, p):
        push((0, slab, z, p), (1, slab, z, p), sib_send.at[(slab * 2 + z) * 4 + p], sib)

    def to_ring2(z, p):
        i = z * 4 + p
        push((0, 0, z, p), (0, 3, z, p), r2_send.at[i], up2)
        push((0, 0, z, p), (0, 1, z, p), r2_send.at[8 + i], dn2)

    def to_ring1(z):
        push((0, 0, z, 0), (0, 0, z, 3), r1_send.at[z], up1)
        push((0, 0, z, 0), (0, 0, z, 1), r1_send.at[2 + z], dn1)

    def got(plane, slab, z, p):
        arrived(piece(plane, slab, z, p), ag_sem(plane, slab, z, p))

    push((0, 0, 0, 0), (0, 0, 1, 0), z_send, zpart)
    to_ring1(0)
    to_ring2(0, 0)
    to_sib(0, 0, 0)
    got(0, 0, 1, 0)
    to_ring1(1)
    to_ring2(1, 0)
    to_sib(0, 1, 0)
    order = [(0, 0), (1, 0), (0, 3), (0, 1), (1, 1), (1, 3), (0, 2), (1, 2)]
    for z, p in order[2:]:
        got(0, 0, z, p)
        if (z, p) == (0, 3):
            push((0, 0, 0, 3), (0, 0, 0, 2), r1_send.at[4], up1)
        if (z, p) == (1, 1):
            push((0, 0, 1, 1), (0, 0, 1, 2), r1_send.at[5], dn1)
        to_ring2(z, p)
        to_sib(0, z, p)
    for z, p in order:
        got(0, 3, z, p)
        if z == 0:
            push((0, 3, 0, p), (0, 2, 0, p), r2_send.at[16 + p], up2)
        to_sib(3, z, p)
        got(0, 1, z, p)
        if z == 1:
            push((0, 1, 1, p), (0, 2, 1, p), r2_send.at[20 + p], dn2)
        to_sib(1, z, p)

    def unfold(plane, lo, hi):
        @pl.loop(lo, hi)
        def _(g):
            rows_at = pl.ds(pl.multiple_of(plane * PLANE_TOK + g * 16, 16), 16)
            for i, dst in ((0, xv), (1, gv)):
                v = ag[i, plane, pl.ds(pl.multiple_of(g * 256, 256), 256), :]
                r = dot(perm[...], v).astype(BF16)
                for k in range(KC):
                    dst[rows_at, k * LC : (k + 1) * LC] = r[16 * k : 16 * k + 16]

    unfold(0, 0, 3)
    for z, p in order:
        got(0, 2, z, p)
        to_sib(2, z, p)
    unfold(0, 3, 6)
    for slab in (0, 3, 1, 2):
        for z, p in order:
            got(1, slab, z, p)
        if slab == 1:
            unfold(1, 0, 3)
    unfold(1, 3, 6)

    load_g.wait()
    load_u.wait()
    load_d.wait()
    gu = dot(xv[...], wgu[...]) * scale_in
    gate, up = gu[:, :HID], gu[:, HID:]
    d_hidden = dot(gv[...], wdn[...]) * scale_hid
    sigma = jax.nn.sigmoid(gate)
    active = gate * sigma
    hidden = (active * up).astype(BF16)
    d_gate = (d_hidden * up * (sigma + gate * sigma * (1.0 - sigma))).astype(BF16)
    d_up = (d_hidden * active).astype(BF16)
    d_gu = jnp.concatenate([d_gate, d_up], axis=1)

    def back(plane):
        lo = plane * PLANE_TOK
        h = hidden[lo : lo + PLANE_TOK]
        dg = d_gu[lo : lo + PLANE_TOK]
        for k in range(KC):
            w = pl.ds(k * LC, LC)
            yv[0, k] = (dot(h, wdn[w, :], NT) * scale_hid).astype(BF16)
            yv[1, k] = (dot(dg, wgu[w, :], NT) * scale_in).astype(BF16)

    def refold(plane, lo, hi):
        @pl.loop(lo, hi)
        def _(g):
            at = pl.ds(pl.multiple_of(g * 16, 16), 16)
            for i in range(2):
                v = yv[i, :, at, :].reshape(256, LC)
                rb[i, plane, pl.ds(pl.multiple_of(g * 256, 256), 256), :] = dot(
                    perm[...], v
                ).astype(BF16)

    def region(ref, lo, n):
        return ref.at[:, pl.ds(lo, n), :]

    HALF = 4 * BR

    def rs_to_sib(slab, z):
        i = slab * 2 + z
        src = rb.at[:, 1, pl.ds(row(slab, z, 0), HALF), :]
        dst = region(sb, row(slab, z, 0), HALF)
        pending.append(send(src, dst, rs_sib_send.at[i], rs_sib_recv.at[i], sib))

    back(1)
    refold(1, 3, 6)
    for slab in (2, 3):
        for z in range(2):
            rs_to_sib(slab, z)
    refold(1, 0, 3)
    for slab in (1, 0):
        for z in range(2):
            rs_to_sib(slab, z)
    back(0)
    refold(0, 3, 6)
    refold(0, 0, 3)

    def add_sib(slab, z):
        lo = row(slab, z, 0)
        arrived(region(sb, lo, HALF), rs_sib_recv.at[slab * 2 + z])
        for i in range(2):
            for p in range(4):
                at = pl.ds(lo + p * BR, BR)
                rb[i, 0, at, :] = (rb[i, 0, at, :].astype(F32) + sb[i, at, :].astype(F32)).astype(
                    BF16
                )

    def mine(slab, z, p):
        return rb.at[:, 0, pl.ds(row(slab, z, p), BR), :]

    def send_t2(way, p, to):
        src = mine(2, way, p)
        i = way * 4 + p
        pending.append(
            send(src, region(t2.at[way], p * BR, BR), t2_send.at[i], t2_recv.at[i], to)
        )

    def send_d2(way, slab, z, p, to):
        i = (way * 2 + z) * 4 + p
        dst = region(d2.at[way], (z * 4 + p) * BR, BR)
        pending.append(send(mine(slab, z, p), dst, d2_send.at[i], d2_recv.at[i], to))

    porder = (2, 1, 3, 0)
    add_sib(2, 0)
    for p in porder:
        send_t2(0, p, up2)
    add_sib(2, 1)
    for p in porder:
        send_t2(1, p, dn2)
    add_sib(3, 0)
    for p in porder:
        send_d2(1, 3, 0, p, dn2)
    add_sib(1, 1)
    for p in porder:
        send_d2(0, 1, 1, p, up2)

    which = frag[...]
    per = D // FR
    masks = [one((which >= m * per) & (which < (m + 1) * per)) for m in range(3)]
    left = jnp.zeros((ROWS, FR), BF16)
    for src, off in ((xv, 1.0 - masks[2]), (gv, masks[2])):
        for c in range(per):
            here = one((which == c) | (which == per + c) | (which == 2 * per + c))
            left = left + src[:, c * FR : (c + 1) * FR] * (off * here).astype(BF16)
    right = (
        d_gate * masks[0].astype(BF16)
        + d_up * masks[1].astype(BF16)
        + hidden * masks[2].astype(BF16)
    )
    factor = inner_rate * (scale_in * (1.0 - masks[2]) + scale_hid * masks[2])
    load_f.wait()
    fq[...] = dot(left, right, TN) * factor - drfv[...]
    fb[...] = fq[...].astype(BF16)
    for d in range(3):
        at = pl.ds(pl.multiple_of(((rep + d + 1) % 4) * QR, 64), QR)
        pending.append(send(fb.at[at, :], fr.at[d], q_send.at[d], q_recv.at[d], reps[d]))

    add_sib(1, 0)
    add_sib(3, 1)

    def add_into(slab, z, p, *others):
        at = pl.ds(row(slab, z, p), BR)
        for i in range(2):
            v = rb[i, 0, at, :].astype(F32)
            for ref, lo in others:
                v = v + ref[i, pl.ds(lo, BR), :].astype(F32)
            rb[i, 0, at, :] = v.astype(BF16)

    for p in porder:
        arrived(region(t2.at[0], p * BR, BR), t2_recv.at[p])
        add_into(1, 0, p, (t2.at[0], p * BR))
        send_d2(0, 1, 0, p, up2)
        arrived(region(t2.at[1], p * BR, BR), t2_recv.at[4 + p])
        add_into(3, 1, p, (t2.at[1], p * BR))
        send_d2(1, 3, 1, p, dn2)
    add_sib(0, 0)
    add_sib(0, 1)

    for d in range(3):
        arrived(fr.at[d], q_recv.at[d])
    own = pl.ds(pl.multiple_of(rep * QR, 64), QR)
    total = fq[own, :]
    for d in range(3):
        total = total + fr[d].astype(F32)
    ps[own, :] = (total * 0.25).astype(BF16)
    for d in range(3):
        pending.append(send(ps.at[own, :], ps.at[own, :], p_send.at[d], p_recv.at[d], reps[d]))

    def finish2(z, p):
        lo = (z * 4 + p) * BR
        for way in range(2):
            arrived(region(d2.at[way], lo, BR), d2_recv.at[(way * 2 + z) * 4 + p])
        add_into(0, z, p, (d2.at[0], lo), (d2.at[1], lo))

    def send_t1(way, to):
        pending.append(
            send(mine(0, way, 2), t1.at[way], t1_send.at[way], t1_recv.at[way], to)
        )

    def send_d1(way, z, p, to):
        i = way * 2 + z
        dst = region(d1.at[way], z * BR, BR)
        pending.append(send(mine(0, z, p), dst, d1_send.at[i], d1_recv.at[i], to))

    finish2(0, 2)
    send_t1(0, up1)
    finish2(1, 2)
    send_t1(1, dn1)
    finish2(1, 1)
    send_d1(0, 1, 1, up1)
    finish2(0, 3)
    send_d1(1, 0, 3, dn1)
    finish2(0, 1)
    arrived(t1.at[0], t1_recv.at[0])
    add_into(0, 0, 1, (t1.at[0], 0))
    send_d1(0, 0, 1, up1)
    finish2(1, 3)
    arrived(t1.at[1], t1_recv.at[1])
    add_into(0, 1, 3, (t1.at[1], 0))
    send_d1(1, 1, 3, dn1)
    finish2(1, 0)
    finish2(0, 0)

    def finish1(z):
        for way in range(2):
            arrived(region(d1.at[way], z * BR, BR), d1_recv.at[way * 2 + z])
        add_into(0, z, 0, (d1.at[0], z * BR), (d1.at[1], z * BR))

    finish1(1)
    pending.append(send(mine(0, 1, 0), zr, zr_send, zr_recv, zpart))

    for d in range(3):
        at = pl.ds(pl.multiple_of(((rep + 3 - d) % 4) * QR, 64), QR)
        arrived(ps.at[at, :], p_recv.at[d])
    out_pseudo[...] = ps[...]

    finish1(0)
    arrived(zr, zr_recv)
    y = rb[0, 0, 0:BR, :].astype(F32) + zr[0].astype(F32)
    dx = rb[1, 0, 0:BR, :].astype(F32) + zr[1].astype(F32)
    d_prob = jnp.sum((gsel * y).reshape(CAP, KC, LC), axis=(1, 2), keepdims=True)
    d_prob = jnp.broadcast_to(d_prob, (CAP, KC, LC)).reshape(BR, LC)
    d_logit = d_prob * prob * (1.0 - prob)
    out_rows[0] = (prob * y).astype(BF16)
    out_rows[1] = (dx + (d_logit * scale_in) * differ).astype(BF16)

    for c in pending:
        c.wait_send()


def finish(
    ids, rows_hbm, pseudo_hbm, params, momentum,
    out_mixed, out_grad, out_params, out_momentum,
    rows, pseudo, mixv, grdv, parv, momv, sem,
):
    def store(src, dst, i):
        c = pltpu.make_async_copy(src, dst, sem.at[i])
        c.start()
        return c

    load_pseudo = store(pseudo_hbm, pseudo, 4)
    load_rows = store(rows_hbm, rows, 5)
    load_pseudo.wait()
    shift = pseudo[...].astype(F32)
    mom = momentum_decay * momentum[...] + shift
    momv[...] = mom
    stores = [store(momv, out_momentum, 0)]
    parv[...] = params[...] - outer_rate * (shift + momentum_decay * mom)
    stores.append(store(parv, out_params, 1))

    rows8 = id_rows(ids)
    tri = one(iota((TOK, TOK), 0) >= iota((TOK, TOK), 1)).astype(BF16)
    eye = one(iota((TOK, TOK), 0) == iota((TOK, TOK), 1)).astype(BF16)
    slot = dot(tri, rows8, NT)[:, 0:1] - 1.0
    routed = dot(eye, rows8, NT)[:, 0:1]
    shape = (TOK, BR)
    mine = (slot == (iota(shape, 1) // KC).astype(F32)) & (routed > 0.5)
    spread = jnp.concatenate(
        [one(mine & (iota(shape, 1) % KC == k)).astype(BF16) for k in range(KC)], axis=0
    )
    load_rows.wait()
    for src, buf, dst in ((0, mixv, out_mixed), (1, grdv, out_grad)):
        placed = dot(spread, rows[src]).astype(BF16)
        for k in range(KC):
            buf[:, k * LC : (k + 1) * LC] = placed[k * TOK : (k + 1) * TOK]
        stores.append(store(buf, dst, 2 + src))
    for c in stores:
        c.wait()


def body(
    tokens,
    expert_ids,
    router_weight,
    expert_weights,
    outer_params,
    outer_momentum,
    inner_drift,
    frag_index,
    out_grad,
):
    vmem = pl.BlockSpec(memory_space=pltpu.VMEM)
    anyw = pl.BlockSpec(memory_space=pl.ANY)
    dma = pltpu.SemaphoreType.DMA
    scratch = [
        pltpu.VMEM((TOK, D), BF16),
        pltpu.VMEM((TOK, D), BF16),
        pltpu.VMEM((D, 2 * HID), BF16),
        pltpu.VMEM((D, HID), BF16),
        pltpu.VMEM((FR, HID), F32),
        pltpu.VMEM((256, 256), BF16),
        pltpu.VMEM((2, 2, PLANE_TOK * KC, LC), BF16),
        pltpu.VMEM((ROWS, D), BF16),
        pltpu.VMEM((ROWS, D), BF16),
        pltpu.VMEM((2, KC, PLANE_TOK, LC), BF16),
        pltpu.VMEM((2, 2, PLANE_TOK * KC, LC), BF16),
        pltpu.VMEM((2, PLANE_TOK * KC, LC), BF16),
        pltpu.VMEM((2, 2, 4 * BR, LC), BF16),
        pltpu.VMEM((2, 2, 8 * BR, LC), BF16),
        pltpu.VMEM((2, 2, BR, LC), BF16),
        pltpu.VMEM((2, 2, 2 * BR, LC), BF16),
        pltpu.VMEM((2, BR, LC), BF16),
        pltpu.VMEM((FR, HID), F32),
        pltpu.VMEM((FR, HID), BF16),
        pltpu.VMEM((3, QR, HID), BF16),
        pltpu.VMEM((FR, HID), BF16),
        dma((6,)),
        dma((64,)),
        dma,
        dma((6,)),
        dma((24,)),
        dma((32,)),
        dma((8,)),
        dma((8,)),
        dma((8,)),
        dma((8,)),
        dma((16,)),
        dma((16,)),
        dma((2,)),
        dma((2,)),
        dma((4,)),
        dma((4,)),
        dma,
        dma,
        dma((3,)),
        dma((3,)),
        dma((3,)),
        dma((3,)),
    ]
    ids = expert_ids.T
    rows, pseudo = pl.pallas_call(
        kernel,
        out_shape=(
            jax.ShapeDtypeStruct((2, BR, LC), BF16),
            jax.ShapeDtypeStruct((FR, HID), BF16),
        ),
        in_specs=[anyw, vmem, vmem, anyw, anyw, vmem, anyw],
        out_specs=(vmem, vmem),
        scratch_shapes=scratch,
        compiler_params=pltpu.CompilerParams(
            collective_id=0, has_side_effects=True, vmem_limit_bytes=56 * 1024 * 1024
        ),
        cost_estimate=pl.CostEstimate(
            flops=4_000_000_000, bytes_accessed=12_000_000, transcendentals=100_000
        ),
    )(
        tokens,
        ids,
        router_weight,
        expert_weights,
        inner_drift,
        frag_index.reshape(1, 1),
        out_grad,
    )
    return pl.pallas_call(
        finish,
        out_shape=(
            jax.ShapeDtypeStruct((TOK, D), BF16),
            jax.ShapeDtypeStruct((TOK, D), BF16),
            jax.ShapeDtypeStruct((FR, HID), F32),
            jax.ShapeDtypeStruct((FR, HID), F32),
        ),
        in_specs=[vmem, anyw, anyw, vmem, vmem],
        out_specs=(anyw, anyw, anyw, anyw),
        scratch_shapes=[
            pltpu.VMEM((2, BR, LC), BF16),
            pltpu.VMEM((FR, HID), BF16),
            pltpu.VMEM((TOK, D), BF16),
            pltpu.VMEM((TOK, D), BF16),
            pltpu.VMEM((FR, HID), F32),
            pltpu.VMEM((FR, HID), F32),
            dma((6,)),
        ],
        compiler_params=pltpu.CompilerParams(vmem_limit_bytes=16 * 1024 * 1024),
    )(ids, rows, pseudo, outer_params, outer_momentum)


def solution(mesh):
    in_specs = (
        P(("replica", "fsdp"), None),
        P(("replica", "fsdp"), None),
        P("replica", None, None),
        P("replica", None, None, "fsdp"),
        P(None, "fsdp"),
        P(None, "fsdp"),
        P("replica", None, "fsdp"),
        P(),
        P(("replica", "fsdp"), None),
    )
    out_specs = (
        P(("replica", "fsdp"), None),
        P(("replica", "fsdp"), None),
        P(None, "fsdp"),
        P(None, "fsdp"),
    )
    return jax.shard_map(body, mesh=mesh, in_specs=in_specs, out_specs=out_specs, check_vma=False)
```

time: 895 us -> 70.3 us (0.08); the launches traced: 879 us -> 70.1 us
  waiting for transfers between devices: 811 us -> 0 us
  Pallas kernels: 0 us -> 66.9 us
  matrix products: 33.7 us -> 0 us
  between operations: 15.2 us -> 1.34 us
  local copies, waits for them, and re-layouts: 13.5 us -> 1.82 us
    unnamed x5 -> x0, waiting for transfers between devices: 567 us -> none
    all_gather x2 -> x0, waiting for transfers between devices: 204 us -> none  [the longest x1 105 us: body(): lax.all_gather(rows_in, 'fsdp', axis=0, tiled=True)]
    pallas_call x0 -> x2, Pallas kernels: none -> 66.9 us  [the longest x1 64.7 us: body(): pl.pallas_call(kernel, out_shape=(jax.ShapeDtypeStruct((2, BR, LC), BF16)...]
    psum x1 -> x0, waiting for transfers between devices: 40.2 us -> none  [body(): total = lax.psum(step_part - drift, 'replica')]
    dot_general x13 -> x0, matrix products: 33.7 us -> none  [the longest x1 5.73 us: body(): lax.dot_general(d_up, w_up, contract, preferred_element_type=jnp.float32)]
    unnamed x17 -> x10, local copies, waits for them, and re-layouts: 13.4 us -> 1.82 us
  transfers between devices with their start and end apart: 4 -> 0, of which waited for: 4 -> 0; matrix products, arithmetic and copies ran while one was open for 3% -> 0% of each run, Pallas kernels for 0% -> 0%
where the time goes in v1:
time: 70.3 us; the launch traced here: 70.1 us
  Pallas kernels  66.9 us (95%)
  local copies, waits for them, and re-layouts  1.82 us (3%)
  between operations  1.34 us (2%)
    pallas_call x1, Pallas kernels, body(): pl.pallas_call(kernel, out_shape=(jax.ShapeDtypeStruct((2, BR, LC), BF16)...  64.7 us
    pallas_call x1, Pallas kernels, body(): pl.pallas_call(finish, out_shape=(jax.ShapeDtypeStruct((TOK, D), BF16), j...  2.23 us
    unnamed x10, local copies, waits for them, and re-layouts  1.82 us

profile of v1, /device:TPU:6, one launch (start us, length us, event | category | flops | bytes accessed | tf_op | source)
XLA Modules:
  0.0 70.1 jit_solution(8572280925011779013)
XLA Ops:
  1.3 0.0 copy-start
  1.3 0.0 copy-start.1
  1.3 0.0 copy-start.4
  1.3 64.7 %shard_map.120 = (bf16[2,48,384]{2,1,0:T(8,128)(2,1)}, bf16[768,128]{1,0:T(8,128)(2,1)}) custom-call(bf16[64,6144]{1,0:T(8,128)(2,1)} %tokens.1, s32[2,64]{1,0:T(2,128)} %bitcast.3, bf16[1,8,6144]{2,1,0:T(8,128)(2,1)} %router.1, bf16[1,3,6144,128]{3,2,1,0:T(8,128)(2,1)} %weights.1, f32[1,768,128]{2,1,0:T(8,128)} %drift.1, s32[1,1]{1,0:T(1,128)} %bitcast.2.frag, ...), custom_call_target="tpu_custom_call" | custom-call | flops 4000000000 | bytes 12000000 | tf_op jit(solution)/shard_map/pallas_call | solution.py:601
  66.0 0.0 copy-done
  66.0 0.0 copy-done.1
  66.0 0.0 copy-done.4
  66.0 0.0 copy-start.2
  66.1 0.9 %copy-done.2 = bf16[768,128]{1,0:T(8,128)(2,1)S(1)} copy-done((bf16[768,128]{1,0:T(8,128)(2,1)S(1)}, bf16[768,128]{1,0:T(8,128)(2,1)}, u32[]{:S(2)}) %copy-start.2) | copy-done | bytes 196632
  67.0 0.0 copy-start.3
  67.0 0.9 %copy-done.3 = bf16[2,48,384]{2,1,0:T(8,128)(2,1)S(1)} copy-done((bf16[2,48,384]{2,1,0:T(8,128)(2,1)S(1)}, bf16[2,48,384]{2,1,0:T(8,128)(2,1)}, u32[]{:S(2)}) %copy-start.3) | copy-done | bytes 73752
  67.9 2.2 %shard_map.121 = (bf16[64,6144]{1,0:T(8,128)(2,1)}, bf16[64,6144]{1,0:T(8,128)(2,1)}, f32[768,128]{1,0:T(8,128)}, f32[768,128]{1,0:T(8,128)}) custom-call(s32[2,64]{1,0:T(2,128)S(1)} %bitcast.4, bf16[2,48,384]{2,1,0:T(8,128)(2,1)S(1)} %copy-done.3, bf16[768,128]{1,0:T(8,128)(2,1)S(1)} %copy-done.2, f32[768,128]{1,0:T(8,128)S(1)} %copy-done, ...), custom_call_target="tpu_custom_call" | custom-call | tf_op jit(solution)/shard_map/pallas_call | solution.py:625
Async XLA Ops:
  1.3 64.7 %copy-start = (f32[768,128]{1,0:T(8,128)S(1)}, f32[768,128]{1,0:T(8,128)}, u32[]{:S(2)}) copy-start(f32[768,128]{1,0:T(8,128)} %params.1) | copy-start | bytes 1179652
  1.3 64.7 %copy-start.1 = (f32[768,128]{1,0:T(8,128)S(1)}, f32[768,128]{1,0:T(8,128)}, u32[]{:S(2)}) copy-start(f32[768,128]{1,0:T(8,128)} %momentum.1) | copy-start | bytes 1179652
  1.3 64.7 %copy-start.4 = (s32[64,2]{0,1:T(2,128)S(1)}, s32[64,2]{0,1:T(2,128)}, u32[]{:S(2)}) copy-start(s32[64,2]{0,1:T(2,128)} %param.10) | copy-start | bytes 1540
  66.0 0.9 %copy-start.2 = (bf16[768,128]{1,0:T(8,128)(2,1)S(1)}, bf16[768,128]{1,0:T(8,128)(2,1)}, u32[]{:S(2)}) copy-start(bf16[768,128]{1,0:T(8,128)(2,1)} %get-tuple-element.7.pseudo_hbm) | copy-start | bytes 589828
  67.0 0.9 %copy-start.3 = (bf16[2,48,384]{2,1,0:T(8,128)(2,1)S(1)}, bf16[2,48,384]{2,1,0:T(8,128)(2,1)}, u32[]{:S(2)}) copy-start(bf16[2,48,384]{2,1,0:T(8,128)(2,1)} %get-tuple-element.6.rows_hbm) | copy-start | bytes 221188

commit v2 on v1

v2 whole, which is shorter than its diff:
```python
import math

import jax
import jax.numpy as jnp
from jax import lax
from jax.experimental import pallas as pl
from jax.experimental.pallas import tpu as pltpu
from jax.sharding import PartitionSpec as P

D = 6144
FF = 8192
EXPERTS = 8
CAP = 3
FR = 768
TOK = 64
KC = 16
LC = D // KC
BR = CAP * KC
NX = 4
NY = 4
NZ = 2
HID = 128
ROWS = 96
QR = FR // 4

inner_rate = 2.0
outer_rate = 0.7
momentum_decay = 0.9
scale_in = 1.0 / math.sqrt(D)
scale_hid = 1.0 / math.sqrt(FF)

MESH = pl.DeviceIdType.MESH
F32 = jnp.float32
BF16 = jnp.bfloat16
NT = (((1,), (1,)), ((), ()))
TN = (((0,), (0,)), ((), ()))


def dot(a, b, dims=(((1,), (0,)), ((), ()))):
    return lax.dot_general(a, b, dims, preferred_element_type=F32)


def iota(shape, dim):
    return lax.broadcasted_iota(jnp.int32, shape, dim)


def one(mask):
    return jnp.where(mask, 1.0, 0.0)


def row(slab, z, p):
    return ((slab * NZ + z) * 4 + p) * BR


def id_rows(ids):
    id0, id1 = ids[0:1, :], ids[1:2, :]
    at = iota((16, TOK), 0)
    routed = one((id0 == 0) | (id1 == 0))
    other = (id0 + id1).astype(F32)
    return jnp.where(at == 0, routed, jnp.where(at == 1, other, 0.0)).astype(BF16)


def kernel(
    tokens,
    ids,
    router,
    weights,
    drift,
    frag,
    grads,
    out_rows,
    out_pseudo,
    tokv,
    grdv,
    wgu,
    wdn,
    drfv,
    perm,
    ag,
    xv,
    gv,
    yv,
    rb,
    t2,
    d2,
    e1,
    fq,
    fb,
    fs,
    fh,
    fr,
    ps,
    load_sem,
    ag_recv,
    r1_send,
    r2_send,
    w_send,
    w_recv,
    t2_send,
    t2_recv,
    d2_send,
    d2_recv,
    e1_send,
    e1_recv,
    f_send,
    f_recv,
    q_send,
    q_recv,
    p_send,
    p_recv,
):
    rep = lax.axis_index("replica")
    me = lax.axis_index("fsdp")
    core = me % 2
    py = (me // 2) % NY
    px = (me // (2 * NY)) % NX
    pz = me // (2 * NY * NX)
    first = 1 - core

    def dev(z, x, y, c):
        return {"fsdp": ((z * NX + x) * NY + y) * 2 + c}

    def at1(z, step):
        x = (px + first * step) % NX
        y = (py + core * step) % NY
        return dev((pz + z) % NZ, x, y, core)

    def at2(step):
        return dev(pz, (px + core * step) % NX, (py + first * step) % NY, core)

    up2, dn2 = at2(1), at2(3)
    sib = dev(pz, px, py, 1 - core)
    near = {(z, p): at1(z, p) for z in range(NZ) for p in range(4) if (z, p) != (0, 0)}
    reps = [{"replica": (rep + d) % 4} for d in (1, 2, 3)]

    def load(src, dst, i):
        c = pltpu.make_async_copy(src, dst, load_sem.at[i])
        c.start()
        return c

    load_tok = load(tokens, tokv, 0)
    load_grd = load(grads, grdv, 1)

    barrier = pltpu.get_barrier_semaphore()
    peers = [up2, dn2, sib] + list(near.values()) + reps
    for p in peers:
        pl.semaphore_signal(barrier, inc=1, device_id=p, device_id_type=MESH)

    def send(src, dst, ssem, rsem, to):
        c = pltpu.make_async_remote_copy(
            src_ref=src, dst_ref=dst, send_sem=ssem, recv_sem=rsem,
            device_id=to, device_id_type=MESH,
        )
        c.start()
        return c

    def arrived(dst, rsem):
        pltpu.make_async_copy(dst, dst, rsem).wait()

    pending = []

    rows8 = id_rows(ids)
    wide = (TOK, KC * TOK)
    tiled = dot(rows8, one(iota(wide, 0) == iota(wide, 1) % TOK).astype(BF16))
    count = dot(rows8, one(iota(wide, 0) <= iota(wide, 1) % TOK).astype(BF16))
    sshape = (BR, KC * TOK)
    smask = (
        (tiled[0:1] > 0.5)
        & (count[0:1] - 1.0 == (iota(sshape, 0) // KC).astype(F32))
        & (iota(sshape, 0) % KC == iota(sshape, 1) // TOK)
    )
    select = one(smask).astype(BF16)
    other48 = jnp.sum(jnp.where(smask, tiled[1:2], 0.0), axis=1, keepdims=True)
    dshape = (BR, KC * EXPERTS)
    expert = iota(dshape, 1) % EXPERTS
    signs = jnp.where(
        iota(dshape, 0) % KC == iota(dshape, 1) // EXPERTS,
        one(expert == 0) - one(expert.astype(F32) == other48),
        0.0,
    ).astype(BF16)
    rw = router[0].astype(F32)
    router2 = jnp.concatenate([rw[:, k * LC : (k + 1) * LC] for k in range(KC)], axis=0)
    differ = dot(signs, router2.astype(BF16))

    pshape = (256, 256)
    perm[...] = one(
        (iota(pshape, 0) // 16 == iota(pshape, 1) % 16)
        & (iota(pshape, 0) % 16 == iota(pshape, 1) // 16)
    ).astype(BF16)

    def fold(ref):
        stacked = jnp.concatenate([ref[:, k * LC : (k + 1) * LC] for k in range(KC)], axis=0)
        return dot(select, stacked)

    load_tok.wait()
    xsel = fold(tokv)
    ag[0, 0:BR, :] = xsel.astype(BF16)
    logit = jnp.sum((xsel * differ).reshape(CAP, KC, LC), axis=(1, 2), keepdims=True)
    prob = jax.nn.sigmoid(jnp.broadcast_to(logit * scale_in, (CAP, KC, LC)).reshape(BR, LC))
    load_grd.wait()
    gsel = fold(grdv)
    ag[1, 0:BR, :] = (prob * gsel).astype(BF16)

    pl.semaphore_wait(barrier, len(peers))

    def piece(ref, slab, z, p):
        return ref.at[:, pl.ds(row(slab, z, p), BR), :]

    def ag_sem(slab, z, p):
        return ag_recv.at[(slab * 2 + z) * 4 + p]

    def push(src_key, dst_key, ssem, to):
        pending.append(send(piece(ag, *src_key), piece(ag, *dst_key), ssem, ag_sem(*dst_key), to))

    def to_ring2(z, p):
        i = z * 4 + p
        push((0, z, p), (3, z, p), r2_send.at[i], up2)
        push((0, z, p), (1, z, p), r2_send.at[8 + i], dn2)

    def got(slab, z, p):
        arrived(piece(ag, slab, z, p), ag_sem(slab, z, p))

    order = [(1, 0), (0, 3), (0, 1), (1, 1), (1, 3), (0, 2), (1, 2)]
    for z, p in order:
        push((0, 0, 0), (0, z, (4 - p) % 4), r1_send.at[z * 4 + p], near[z, p])
    to_ring2(0, 0)

    loads = []
    for m, (dst, lo, far) in enumerate(((wgu, 0, 2 * HID), (wgu, HID, 3 * HID), (wdn, 0, HID))):
        src = weights.at[0, m]
        loads.append(load(src, dst.at[:, lo : lo + HID], 2 + m))
        pending.append(send(src, dst.at[:, far : far + HID], w_send.at[m], w_recv.at[m], sib))
    load_f = load(drift.at[0], drfv, 5)

    for z, p in order:
        got(0, z, p)
        to_ring2(z, p)

    def unfold(lo, hi):
        @pl.loop(lo, hi)
        def _(g):
            rows_at = pl.ds(pl.multiple_of(g * 16, 16), 16)
            for i, dst in ((0, xv), (1, gv)):
                v = ag[i, pl.ds(pl.multiple_of(g * 256, 256), 256), :]
                r = dot(perm[...], v).astype(BF16)
                for k in range(KC):
                    dst[rows_at, k * LC : (k + 1) * LC] = r[16 * k : 16 * k + 16]

    for z, p in [(0, 0)] + order:
        got(3, z, p)
        if z == 0:
            push((3, 0, p), (2, 0, p), r2_send.at[16 + p], up2)
        got(1, z, p)
        if z == 1:
            push((1, 1, p), (2, 1, p), r2_send.at[20 + p], dn2)
    unfold(0, 3)
    for z, p in [(0, 0)] + order:
        got(2, z, p)
    unfold(3, 6)

    for c in loads:
        c.wait()
    for m, (dst, far) in enumerate(((wgu, 2 * HID), (wgu, 3 * HID), (wdn, HID))):
        arrived(dst.at[:, far : far + HID], w_recv.at[m])
    gu = dot(xv[...], wgu[...]) * scale_in
    gate = jnp.concatenate([gu[:, 0:HID], gu[:, 2 * HID : 3 * HID]], axis=1)
    up = jnp.concatenate([gu[:, HID : 2 * HID], gu[:, 3 * HID :]], axis=1)
    d_hidden = dot(gv[...], wdn[...]) * scale_hid
    sigma = jax.nn.sigmoid(gate)
    active = gate * sigma
    hidden = (active * up).astype(BF16)
    d_gate = (d_hidden * up * (sigma + gate * sigma * (1.0 - sigma))).astype(BF16)
    d_up = (d_hidden * active).astype(BF16)
    d_gu = jnp.concatenate(
        [d_gate[:, :HID], d_up[:, :HID], d_gate[:, HID:], d_up[:, HID:]], axis=1
    )

    for k in range(KC):
        w = pl.ds(k * LC, LC)
        yv[0, k] = (dot(hidden, wdn[w, :], NT) * scale_hid).astype(BF16)
        yv[1, k] = (dot(d_gu, wgu[w, :], NT) * scale_in).astype(BF16)

    def refold(lo, hi):
        @pl.loop(lo, hi)
        def _(g):
            at = pl.ds(pl.multiple_of(g * 16, 16), 16)
            for i in range(2):
                v = yv[i, :, at, :].reshape(256, LC)
                rb[i, pl.ds(pl.multiple_of(g * 256, 256), 256), :] = dot(perm[...], v).astype(BF16)

    def region(ref, lo, n):
        return ref.at[:, pl.ds(lo, n), :]

    def send_t2(way, p, to):
        i = way * 4 + p
        dst = region(t2.at[way], p * BR, BR)
        pending.append(send(piece(rb, 2, way, p), dst, t2_send.at[i], t2_recv.at[i], to))

    def send_d2(way, slab, z, p, to):
        i = (way * 2 + z) * 4 + p
        dst = region(d2.at[way], (z * 4 + p) * BR, BR)
        pending.append(send(piece(rb, slab, z, p), dst, d2_send.at[i], d2_recv.at[i], to))

    porder = (2, 1, 3, 0)
    refold(3, 6)
    for p in porder:
        send_t2(0, p, up2)
        send_t2(1, p, dn2)
    for p in porder:
        send_d2(1, 3, 0, p, dn2)
    refold(0, 3)
    for p in porder:
        send_d2(0, 1, 1, p, up2)

    which = frag[...]
    per = D // FR
    masks = [one((which >= m * per) & (which < (m + 1) * per)) for m in range(3)]
    left = jnp.zeros((ROWS, FR), BF16)
    for src, off in ((xv, 1.0 - masks[2]), (gv, masks[2])):
        for c in range(per):
            here = one((which == c) | (which == per + c) | (which == 2 * per + c))
            left = left + src[:, c * FR : (c + 1) * FR] * (off * here).astype(BF16)
    right = (
        d_gate * masks[0].astype(BF16)
        + d_up * masks[1].astype(BF16)
        + hidden * masks[2].astype(BF16)
    )
    factor = inner_rate * (scale_in * (1.0 - masks[2]) + scale_hid * masks[2])
    partial = dot(left, right, TN) * factor
    fb[...] = partial[:, HID:].astype(BF16)
    pending.append(send(fb, fs, f_send, f_recv, sib))
    load_f.wait()
    fq[...] = partial[:, :HID] - drfv[...]

    def add_into(slab, z, p, *others):
        at = pl.ds(row(slab, z, p), BR)
        for i in range(2):
            v = rb[i, at, :].astype(F32)
            for ref, lo in others:
                v = v + ref[i, pl.ds(lo, BR), :].astype(F32)
            rb[i, at, :] = v.astype(BF16)

    for j, p in enumerate(porder):
        arrived(region(t2.at[0], p * BR, BR), t2_recv.at[p])
        add_into(1, 0, p, (t2.at[0], p * BR))
        send_d2(0, 1, 0, p, up2)
        arrived(region(t2.at[1], p * BR, BR), t2_recv.at[4 + p])
        add_into(3, 1, p, (t2.at[1], p * BR))
        send_d2(1, 3, 1, p, dn2)
        if j == 1:
            arrived(fs, f_recv)
            fq[...] = fq[...] + fs[...].astype(F32)
            fh[...] = fq[...].astype(BF16)
            for d in range(3):
                at = pl.ds(pl.multiple_of(((rep + d + 1) % 4) * QR, 64), QR)
                pending.append(
                    send(fh.at[at, :], fr.at[d], q_send.at[d], q_recv.at[d], reps[d])
                )

    def finish2(z, p):
        lo = (z * 4 + p) * BR
        for way in range(2):
            arrived(region(d2.at[way], lo, BR), d2_recv.at[(way * 2 + z) * 4 + p])
        add_into(0, z, p, (d2.at[0], lo), (d2.at[1], lo))
        if (z, p) != (0, 0):
            i = z * 4 + (4 - p) % 4
            pending.append(
                send(piece(rb, 0, z, p), e1.at[i], e1_send.at[i], e1_recv.at[i], near[z, p])
            )

    for j, p in enumerate(porder):
        finish2(1, p)
        finish2(0, p)
        if j == 0:
            for d in range(3):
                arrived(fr.at[d], q_recv.at[d])
            own = pl.ds(pl.multiple_of(rep * QR, 64), QR)
            total = fq[own, :]
            for d in range(3):
                total = total + fr[d].astype(F32)
            ps[own, :] = (total * 0.25).astype(BF16)
            for d in range(3):
                pending.append(
                    send(ps.at[own, :], ps.at[own, :], p_send.at[d], p_recv.at[d], reps[d])
                )

    y = rb[0, 0:BR, :].astype(F32)
    dx = rb[1, 0:BR, :].astype(F32)
    for z, p in [(1, 0), (0, 1), (0, 3), (1, 1), (1, 3), (0, 2), (1, 2)]:
        i = z * 4 + p
        arrived(e1.at[i], e1_recv.at[i])
        y = y + e1[i, 0].astype(F32)
        dx = dx + e1[i, 1].astype(F32)
    d_prob = jnp.sum((gsel * y).reshape(CAP, KC, LC), axis=(1, 2), keepdims=True)
    d_prob = jnp.broadcast_to(d_prob, (CAP, KC, LC)).reshape(BR, LC)
    d_logit = d_prob * prob * (1.0 - prob)
    out_rows[0] = (prob * y).astype(BF16)
    out_rows[1] = (dx + (d_logit * scale_in) * differ).astype(BF16)

    for d in range(3):
        at = pl.ds(pl.multiple_of(((rep + 3 - d) % 4) * QR, 64), QR)
        arrived(ps.at[at, :], p_recv.at[d])
    out_pseudo[...] = ps[...]

    for c in pending:
        c.wait_send()


def finish(
    ids, rows_hbm, pseudo_hbm, params, momentum,
    out_mixed, out_grad, out_params, out_momentum,
    rows, pseudo, mixv, grdv, parv, momv, sem,
):
    def store(src, dst, i):
        c = pltpu.make_async_copy(src, dst, sem.at[i])
        c.start()
        return c

    load_rows = store(rows_hbm, rows, 5)
    loads = [store(pseudo_hbm, pseudo, 4), store(momentum, momv, 6), store(params, parv, 7)]

    rows8 = id_rows(ids)
    tri = one(iota((TOK, TOK), 0) >= iota((TOK, TOK), 1)).astype(BF16)
    eye = one(iota((TOK, TOK), 0) == iota((TOK, TOK), 1)).astype(BF16)
    slot = dot(tri, rows8, NT)[:, 0:1] - 1.0
    routed = dot(eye, rows8, NT)[:, 0:1]
    shape = (TOK, BR)
    mine = (slot == (iota(shape, 1) // KC).astype(F32)) & (routed > 0.5)
    spread = jnp.concatenate(
        [one(mine & (iota(shape, 1) % KC == k)).astype(BF16) for k in range(KC)], axis=0
    )
    stores = []
    load_rows.wait()
    for src, buf, dst in ((0, mixv, out_mixed), (1, grdv, out_grad)):
        placed = dot(spread, rows[src]).astype(BF16)
        for k in range(KC):
            buf[:, k * LC : (k + 1) * LC] = placed[k * TOK : (k + 1) * TOK]
        stores.append(store(buf, dst, 2 + src))
    for c in loads:
        c.wait()
    shift = pseudo[...].astype(F32)
    mom = momentum_decay * momv[...] + shift
    momv[...] = mom
    stores.append(store(momv, out_momentum, 0))
    parv[...] = parv[...] - outer_rate * (shift + momentum_decay * mom)
    stores.append(store(parv, out_params, 1))
    for c in stores:
        c.wait()


def body(
    tokens,
    expert_ids,
    router_weight,
    expert_weights,
    outer_params,
    outer_momentum,
    inner_drift,
    frag_index,
    out_grad,
):
    vmem = pl.BlockSpec(memory_space=pltpu.VMEM)
    anyw = pl.BlockSpec(memory_space=pl.ANY)
    dma = pltpu.SemaphoreType.DMA
    scratch = [
        pltpu.VMEM((TOK, D), BF16),
        pltpu.VMEM((TOK, D), BF16),
        pltpu.VMEM((D, 4 * HID), BF16),
        pltpu.VMEM((D, 2 * HID), BF16),
        pltpu.VMEM((FR, HID), F32),
        pltpu.VMEM((256, 256), BF16),
        pltpu.VMEM((2, ROWS * KC, LC), BF16),
        pltpu.VMEM((ROWS, D), BF16),
        pltpu.VMEM((ROWS, D), BF16),
        pltpu.VMEM((2, KC, ROWS, LC), BF16),
        pltpu.VMEM((2, ROWS * KC, LC), BF16),
        pltpu.VMEM((2, 2, 4 * BR, LC), BF16),
        pltpu.VMEM((2, 2, 8 * BR, LC), BF16),
        pltpu.VMEM((8, 2, BR, LC), BF16),
        pltpu.VMEM((FR, HID), F32),
        pltpu.VMEM((FR, HID), BF16),
        pltpu.VMEM((FR, HID), BF16),
        pltpu.VMEM((FR, HID), BF16),
        pltpu.VMEM((3, QR, HID), BF16),
        pltpu.VMEM((FR, HID), BF16),
        dma((6,)),
        dma((32,)),
        dma((8,)),
        dma((24,)),
        dma((3,)),
        dma((3,)),
        dma((8,)),
        dma((8,)),
        dma((16,)),
        dma((16,)),
        dma((8,)),
        dma((8,)),
        dma,
        dma,
        dma((3,)),
        dma((3,)),
        dma((3,)),
        dma((3,)),
    ]
    ids = expert_ids.T
    rows, pseudo = pl.pallas_call(
        kernel,
        out_shape=(
            jax.ShapeDtypeStruct((2, BR, LC), BF16),
            jax.ShapeDtypeStruct((FR, HID), BF16),
        ),
        in_specs=[anyw, vmem, vmem, anyw, anyw, vmem, anyw],
        out_specs=(vmem, vmem),
        scratch_shapes=scratch,
        compiler_params=pltpu.CompilerParams(
            collective_id=0, has_side_effects=True, vmem_limit_bytes=56 * 1024 * 1024
        ),
        cost_estimate=pl.CostEstimate(
            flops=4_000_000_000, bytes_accessed=12_000_000, transcendentals=100_000
        ),
    )(
        tokens,
        ids,
        router_weight,
        expert_weights,
        inner_drift,
        frag_index.reshape(1, 1),
        out_grad,
    )
    return pl.pallas_call(
        finish,
        out_shape=(
            jax.ShapeDtypeStruct((TOK, D), BF16),
            jax.ShapeDtypeStruct((TOK, D), BF16),
            jax.ShapeDtypeStruct((FR, HID), F32),
            jax.ShapeDtypeStruct((FR, HID), F32),
        ),
        in_specs=[vmem, anyw, anyw, anyw, anyw],
        out_specs=(anyw, anyw, anyw, anyw),
        scratch_shapes=[
            pltpu.VMEM((2, BR, LC), BF16),
            pltpu.VMEM((FR, HID), BF16),
            pltpu.VMEM((TOK, D), BF16),
            pltpu.VMEM((TOK, D), BF16),
            pltpu.VMEM((FR, HID), F32),
            pltpu.VMEM((FR, HID), F32),
            dma((8,)),
        ],
        compiler_params=pltpu.CompilerParams(vmem_limit_bytes=62 * 1024 * 1024),
    )(ids, rows, pseudo, outer_params, outer_momentum)


def solution(mesh):
    in_specs = (
        P(("replica", "fsdp"), None),
        P(("replica", "fsdp"), None),
        P("replica", None, None),
        P("replica", None, None, "fsdp"),
        P(None, "fsdp"),
        P(None, "fsdp"),
        P("replica", None, "fsdp"),
        P(),
        P(("replica", "fsdp"), None),
    )
    out_specs = (
        P(("replica", "fsdp"), None),
        P(("replica", "fsdp"), None),
        P(None, "fsdp"),
        P(None, "fsdp"),
    )
    return jax.shard_map(body, mesh=mesh, in_specs=in_specs, out_specs=out_specs, check_vma=False)
```

time: 70.3 us -> 61.9 us (0.88); the launches traced: 70.1 us -> 60.8 us
  Pallas kernels: 66.9 us -> 59.5 us
  local copies, waits for them, and re-layouts: 1.82 us -> 0 us
    pallas_call x1, Pallas kernels: 64.7 us -> 56.1 us  [body(): pl.pallas_call(kernel, out_shape=(jax.ShapeDtypeStruct((2, BR, LC), BF16)...]
    unnamed x10 -> x0, local copies, waits for them, and re-layouts: 1.82 us -> none
    pallas_call x1, Pallas kernels: 2.23 us -> 3.44 us  [body(): pl.pallas_call(finish, out_shape=(jax.ShapeDtypeStruct((TOK, D), BF16), j...]
where the time goes in v2:
time: 61.9 us; the launch traced here: 60.8 us
  Pallas kernels  59.5 us (96%)
  between operations  1.29 us (2%)
    pallas_call x1, Pallas kernels, body(): pl.pallas_call(kernel, out_shape=(jax.ShapeDtypeStruct((2, BR, LC), BF16)...  56.1 us
    pallas_call x1, Pallas kernels, body(): pl.pallas_call(finish, out_shape=(jax.ShapeDtypeStruct((TOK, D), BF16), j...  3.44 us

profile of v2, /device:TPU:6, one launch (start us, length us, event | category | flops | bytes accessed | tf_op | source)
XLA Modules:
  0.0 60.8 jit_solution(4694230443970285710)
XLA Ops:
  1.3 56.1 %shard_map.120 = (bf16[2,48,384]{2,1,0:T(8,128)(2,1)}, bf16[768,128]{1,0:T(8,128)(2,1)}) custom-call(bf16[64,6144]{1,0:T(8,128)(2,1)} %tokens.1, s32[2,64]{1,0:T(2,128)} %bitcast.3, bf16[1,8,6144]{2,1,0:T(8,128)(2,1)} %router.1, bf16[1,3,6144,128]{3,2,1,0:T(8,128)(2,1)} %weights.1, f32[1,768,128]{2,1,0:T(8,128)} %drift.1, s32[1,1]{1,0:T(1,128)} %bitcast.2.frag, ...), custom_call_target="tpu_custom_call" | custom-call | flops 4000000000 | bytes 12000000 | tf_op jit(solution)/shard_map/pallas_call | solution.py:506
  57.4 3.4 %shard_map.121 = (bf16[64,6144]{1,0:T(8,128)(2,1)}, bf16[64,6144]{1,0:T(8,128)(2,1)}, f32[768,128]{1,0:T(8,128)}, f32[768,128]{1,0:T(8,128)}) custom-call(s32[2,64]{1,0:T(2,128)} %bitcast.4, bf16[2,48,384]{2,1,0:T(8,128)(2,1)} %get-tuple-element.6.rows_hbm, bf16[768,128]{1,0:T(8,128)(2,1)} %get-tuple-element.7.pseudo_hbm, f32[768,128]{1,0:T(8,128)} %params.1, ...), custom_call_target="tpu_custom_call" | custom-call | tf_op jit(solution)/shard_map/pallas_call | solution.py:530

commit v3 on v2

v3 whole, which is shorter than its diff:
```python
import math

import jax
import jax.numpy as jnp
from jax import lax
from jax.experimental import pallas as pl
from jax.experimental.pallas import tpu as pltpu
from jax.sharding import PartitionSpec as P

D = 6144
FF = 8192
EXPERTS = 8
CAP = 3
FR = 768
TOK = 64
KC = 16
LC = D // KC
BR = CAP * KC
NX = 4
NY = 4
NZ = 2
HID = 128
ROWS = 96
QR = FR // 4
HR = QR // 2

inner_rate = 2.0
outer_rate = 0.7
momentum_decay = 0.9
scale_in = 1.0 / math.sqrt(D)
scale_hid = 1.0 / math.sqrt(FF)

MESH = pl.DeviceIdType.MESH
F32 = jnp.float32
BF16 = jnp.bfloat16
NT = (((1,), (1,)), ((), ()))
TN = (((0,), (0,)), ((), ()))


def dot(a, b, dims=(((1,), (0,)), ((), ()))):
    return lax.dot_general(a, b, dims, preferred_element_type=F32)


def iota(shape, dim):
    return lax.broadcasted_iota(jnp.int32, shape, dim)


def one(mask):
    return jnp.where(mask, 1.0, 0.0)


POS = (0, 1, 3, 2)
GROUP = ((0, 1), (1, 2), (3, 1))
MEMBERS = ((0,), (1, 3), (2,))


def row(slab, z, p):
    return ((slab * NZ + z) * 4 + POS[p]) * BR


def group_rows(slab, z, g):
    return pl.ds(((slab * NZ + z) * 4 + GROUP[g][0]) * BR, GROUP[g][1] * BR)


def id_rows(ids):
    id0, id1 = ids[0:1, :], ids[1:2, :]
    at = iota((16, TOK), 0)
    routed = one((id0 == 0) | (id1 == 0))
    other = (id0 + id1).astype(F32)
    return jnp.where(at == 0, routed, jnp.where(at == 1, other, 0.0)).astype(BF16)


def kernel(
    tokens,
    ids_hbm,
    router_hbm,
    weights,
    drift,
    frag_hbm,
    grads,
    out_rows,
    out_pseudo,
    ids,
    router,
    frag,
    tokv,
    grdv,
    wgu,
    wdn,
    drfv,
    perm,
    ag,
    xv,
    gv,
    yv,
    rb,
    t2,
    d2,
    e1,
    fq,
    fb,
    fs,
    fh,
    fr,
    ps,
    load_sem,
    n_send,
    n_recv,
    r_send,
    r_recv,
    w_send,
    w_recv,
    t2_send,
    t2_recv,
    d2_send,
    d2_recv,
    e1_send,
    e1_recv,
    f_send,
    f_recv,
    q_send,
    q_recv,
    p_send,
    p_recv,
):
    rep = lax.axis_index("replica")
    me = lax.axis_index("fsdp")
    core = me % 2
    py = (me // 2) % NY
    px = (me // (2 * NY)) % NX
    pz = me // (2 * NY * NX)
    first = 1 - core

    def dev(z, x, y, c):
        return {"fsdp": ((z * NX + x) * NY + y) * 2 + c}

    def at1(z, step):
        x = (px + first * step) % NX
        y = (py + core * step) % NY
        return dev((pz + z) % NZ, x, y, core)

    def at2(step):
        return dev(pz, (px + core * step) % NX, (py + first * step) % NY, core)

    up2, dn2 = at2(1), at2(3)
    sib = dev(pz, px, py, 1 - core)
    near = {(z, p): at1(z, p) for z in range(NZ) for p in range(4) if (z, p) != (0, 0)}
    reps = [{"replica": (rep + d) % 4} for d in (1, 2, 3)]

    def load(src, dst, i):
        c = pltpu.make_async_copy(src, dst, load_sem.at[i])
        c.start()
        return c

    load_ids = load(ids_hbm, ids, 6)
    load_rtr = load(router_hbm, router, 7)
    load_frag = load(frag_hbm, frag, 8)
    load_tok = load(tokens, tokv, 0)
    load_grd = load(grads, grdv, 1)

    barrier = pltpu.get_barrier_semaphore()
    peers = [up2, dn2, sib] + list(near.values()) + reps
    for p in peers:
        pl.semaphore_signal(barrier, inc=1, device_id=p, device_id_type=MESH)

    def send(src, dst, ssem, rsem, to):
        c = pltpu.make_async_remote_copy(
            src_ref=src, dst_ref=dst, send_sem=ssem, recv_sem=rsem,
            device_id=to, device_id_type=MESH,
        )
        c.start()
        return c

    def arrived(dst, rsem):
        pltpu.make_async_copy(dst, dst, rsem).wait()

    pending = []

    load_ids.wait()
    rows8 = id_rows(ids)
    wide = (TOK, KC * TOK)
    tiled = dot(rows8, one(iota(wide, 0) == iota(wide, 1) % TOK).astype(BF16))
    count = dot(rows8, one(iota(wide, 0) <= iota(wide, 1) % TOK).astype(BF16))
    sshape = (BR, KC * TOK)
    smask = (
        (tiled[0:1] > 0.5)
        & (count[0:1] - 1.0 == (iota(sshape, 0) // KC).astype(F32))
        & (iota(sshape, 0) % KC == iota(sshape, 1) // TOK)
    )
    select = one(smask).astype(BF16)
    other48 = jnp.sum(jnp.where(smask, tiled[1:2], 0.0), axis=1, keepdims=True)
    dshape = (BR, KC * EXPERTS)
    expert = iota(dshape, 1) % EXPERTS
    signs = jnp.where(
        iota(dshape, 0) % KC == iota(dshape, 1) // EXPERTS,
        one(expert == 0) - one(expert.astype(F32) == other48),
        0.0,
    ).astype(BF16)
    load_rtr.wait()
    load_frag.wait()
    rw = router[0].astype(F32)
    router2 = jnp.concatenate([rw[:, k * LC : (k + 1) * LC] for k in range(KC)], axis=0)
    differ = dot(signs, router2.astype(BF16))

    pshape = (256, 256)
    perm[...] = one(
        (iota(pshape, 0) // 16 == iota(pshape, 1) % 16)
        & (iota(pshape, 0) % 16 == iota(pshape, 1) // 16)
    ).astype(BF16)

    def fold(ref):
        stacked = jnp.concatenate([ref[:, k * LC : (k + 1) * LC] for k in range(KC)], axis=0)
        return dot(select, stacked)

    load_tok.wait()
    xsel = fold(tokv)
    ag[0, 0:BR, :] = xsel.astype(BF16)

    pl.semaphore_wait(barrier, len(peers))

    def piece(ref, i, slab, z, p):
        return ref.at[i, pl.ds(row(slab, z, p), BR), :]

    def group(ref, i, slab, z, g):
        return ref.at[i, group_rows(slab, z, g), :]

    def put(src, dst, ssem, rsem, to):
        pending.append(send(src, dst, ssem, rsem, to))

    far_last = [(1, 0), (0, 1), (0, 3), (1, 1), (1, 3), (0, 2), (1, 2)]

    def to_near(i):
        for z, p in far_last:
            q = (4 - p) % 4
            put(
                piece(ag, i, 0, 0, 0), piece(ag, i, 0, z, q),
                n_send.at[i, z * 4 + p], n_recv.at[i, z * 4 + q], near[z, p],
            )

    def to_ring(i, z, g):
        j = z * 3 + g
        src = group(ag, i, 0, z, g)
        put(src, group(ag, i, 3, z, g), r_send.at[i, 0, j], r_recv.at[i, 3, j], up2)
        put(src, group(ag, i, 1, z, g), r_send.at[i, 1, j], r_recv.at[i, 1, j], dn2)

    def near_to_ring(z, g):
        for i in range(2):
            for p in MEMBERS[g]:
                arrived(piece(ag, i, 0, z, p), n_recv.at[i, z * 4 + p])
            to_ring(i, z, g)

    def got_ring(i, slab, z, g):
        arrived(group(ag, i, slab, z, g), r_recv.at[i, slab, z * 3 + g])

    def relay(z, g):
        j = z * 3 + g
        for i in range(2):
            got_ring(i, 3, z, g)
            if z == 0:
                src = group(ag, i, 3, z, g)
                put(src, group(ag, i, 2, z, g), r_send.at[i, 2, j], r_recv.at[i, 2, j], up2)
            got_ring(i, 1, z, g)
            if z == 1:
                src = group(ag, i, 1, z, g)
                put(src, group(ag, i, 2, z, g), r_send.at[i, 2, j], r_recv.at[i, 2, j], dn2)

    def unfold(lo, hi):
        @pl.loop(lo, hi, unroll=True)
        def _(g):
            rows_at = pl.ds(pl.multiple_of(g * 16, 16), 16)
            for i, dst in ((0, xv), (1, gv)):
                v = ag[i, pl.ds(pl.multiple_of(g * 256, 256), 256), :]
                r = dot(perm[...], v).astype(BF16)
                for k in range(KC):
                    dst[rows_at, k * LC : (k + 1) * LC] = r[16 * k : 16 * k + 16]

    to_ring(0, 0, 0)
    to_near(0)
    logit = jnp.sum((xsel * differ).reshape(CAP, KC, LC), axis=(1, 2), keepdims=True)
    prob = jax.nn.sigmoid(jnp.broadcast_to(logit * scale_in, (CAP, KC, LC)).reshape(BR, LC))
    load_grd.wait()
    gsel = fold(grdv)
    ag[1, 0:BR, :] = (prob * gsel).astype(BF16)
    to_ring(1, 0, 0)
    to_near(1)

    loads = []
    for m, (dst, lo, far) in enumerate(((wgu, 0, 2 * HID), (wgu, HID, 3 * HID), (wdn, 0, HID))):
        src = weights.at[0, m]
        loads.append(load(src, dst.at[:, lo : lo + HID], 2 + m))
        put(src, dst.at[:, far : far + HID], w_send.at[m], w_recv.at[m], sib)
    loads.append(load(drift.at[0], drfv, 5))

    order = [(0, 0), (1, 0), (0, 1), (1, 1), (0, 2), (1, 2)]
    for z, g in order[1:]:
        near_to_ring(z, g)
    for z, g in order:
        relay(z, g)
    unfold(0, 3)
    for z, g in order:
        got_ring(0, 2, z, g)
        got_ring(1, 2, z, g)
    unfold(3, 6)

    for c in loads:
        c.wait()
    for m, (dst, far) in enumerate(((wgu, 2 * HID), (wgu, 3 * HID), (wdn, HID))):
        arrived(dst.at[:, far : far + HID], w_recv.at[m])
    gu = dot(xv[...], wgu[...]) * scale_in
    gate = jnp.concatenate([gu[:, 0:HID], gu[:, 2 * HID : 3 * HID]], axis=1)
    up = jnp.concatenate([gu[:, HID : 2 * HID], gu[:, 3 * HID :]], axis=1)
    sigma = jax.nn.sigmoid(gate)
    active = gate * sigma
    hidden = (active * up).astype(BF16)
    d_hidden = dot(gv[...], wdn[...]) * scale_hid
    d_gate = (d_hidden * up * (sigma + gate * sigma * (1.0 - sigma))).astype(BF16)
    d_up = (d_hidden * active).astype(BF16)
    d_gu = jnp.concatenate(
        [d_gate[:, :HID], d_up[:, :HID], d_gate[:, HID:], d_up[:, HID:]], axis=1
    )

    which = frag[...]
    per = D // FR
    masks = [one((which >= m * per) & (which < (m + 1) * per)) for m in range(3)]
    left = jnp.zeros((ROWS, FR), BF16)
    for src, off in ((xv, 1.0 - masks[2]), (gv, masks[2])):
        for c in range(per):
            here = one((which == c) | (which == per + c) | (which == 2 * per + c))
            left = left + src[:, c * FR : (c + 1) * FR] * (off * here).astype(BF16)
    right = (
        d_gate * masks[0].astype(BF16)
        + d_up * masks[1].astype(BF16)
        + hidden * masks[2].astype(BF16)
    )
    factor = inner_rate * (scale_in * (1.0 - masks[2]) + scale_hid * masks[2])
    partial = dot(left, right, TN) * factor
    fb[...] = partial[:, HID:].astype(BF16)
    put(fb, fs, f_send, f_recv, sib)
    fq[...] = partial[:, :HID] - drfv[...]

    def back(i, rows_at, w, scale):
        for k in range(KC):
            part = dot(rows_at, w[k * LC : (k + 1) * LC, :], NT)
            yv[i, k] = (part * scale).astype(BF16)

    def refold(i, lo, hi):
        @pl.loop(lo, hi, unroll=True)
        def _(g):
            v = yv[i, :, pl.ds(pl.multiple_of(g * 16, 16), 16), :].reshape(256, LC)
            rb[i, pl.ds(pl.multiple_of(g * 256, 256), 256), :] = dot(perm[...], v).astype(BF16)

    def transit(i, way, g):
        at = pl.ds(GROUP[g][0] * BR, GROUP[g][1] * BR)
        return t2.at[i, way, at, :]

    def landing(i, way, z, g):
        return d2.at[i, way, group_rows(0, z, g), :]

    def send_transit(i, way, g, to):
        put(
            group(rb, i, 2, way, g), transit(i, way, g),
            t2_send.at[i, way, g], t2_recv.at[i, way, g], to,
        )

    def send_landing(i, way, slab, z, g, to):
        j = z * 3 + g
        put(
            group(rb, i, slab, z, g), landing(i, way, z, g),
            d2_send.at[i, way, j], d2_recv.at[i, way, j], to,
        )

    def add_into(i, at, *others):
        v = rb[i, at, :].astype(F32)
        for other in others:
            v = v + other[...].astype(F32)
        rb[i, at, :] = v.astype(BF16)

    def scatter_start(i):
        refold(i, 3, 6)
        for g in (2, 1, 0):
            send_transit(i, 0, g, up2)
            send_transit(i, 1, g, dn2)
        refold(i, 0, 3)

    def scatter_direct(i, g):
        send_landing(i, 0, 1, 1, g, up2)
        send_landing(i, 1, 3, 0, g, dn2)

    def scatter_relay(i, g):
        arrived(transit(i, 0, g), t2_recv.at[i, 0, g])
        add_into(i, group_rows(1, 0, g), transit(i, 0, g))
        send_landing(i, 0, 1, 0, g, up2)
        arrived(transit(i, 1, g), t2_recv.at[i, 1, g])
        add_into(i, group_rows(3, 1, g), transit(i, 1, g))
        send_landing(i, 1, 3, 1, g, dn2)

    def scatter_near(i, g):
        for z in (1, 0):
            for way in range(2):
                arrived(landing(i, way, z, g), d2_recv.at[i, way, z * 3 + g])
            add_into(i, group_rows(0, z, g), landing(i, 0, z, g), landing(i, 1, z, g))
            for p in MEMBERS[g]:
                if (z, p) != (0, 0):
                    j = z * 4 + (4 - p) % 4
                    put(
                        piece(rb, i, 0, z, p), e1.at[i, j],
                        e1_send.at[i, z * 4 + p], e1_recv.at[i, j], near[z, p],
                    )

    def scatter_end(i):
        v = rb[i, 0:BR, :].astype(F32)
        for z, p in far_last:
            j = z * 4 + p
            arrived(e1.at[i, j], e1_recv.at[i, j])
            v = v + e1[i, j].astype(F32)
        return v

    back(0, hidden, wdn, scale_hid)
    arrived(fs, f_recv)
    fq[...] = fq[...] + fs[...].astype(F32)
    fh[...] = fq[...].astype(BF16)

    def half(quarter, h):
        return pl.ds(pl.multiple_of(quarter * QR + h * HR, 32), HR)

    for h in range(2):
        for d in (1, 0, 2):
            at = half((rep + d + 1) % 4, h)
            put(fh.at[at, :], fr.at[d, h], q_send.at[d, h], q_recv.at[d, h], reps[d])

    def sum_quarter(h):
        own = half(rep, h)
        total = fq[own, :]
        for d in range(3):
            arrived(fr.at[d, h], q_recv.at[d, h])
            total = total + fr[d, h].astype(F32)
        ps[own, :] = (total * 0.25).astype(BF16)
        for d in (1, 0, 2):
            put(ps.at[own, :], ps.at[own, :], p_send.at[d, h], p_recv.at[d, h], reps[d])

    scatter_start(0)
    for g in (2, 1, 0):
        scatter_direct(0, g)
    back(1, d_gu, wgu, scale_in)
    scatter_start(1)
    for g in (2, 1, 0):
        scatter_relay(0, g)
    scatter_direct(1, 2)
    scatter_relay(1, 2)
    scatter_direct(1, 1)
    scatter_relay(1, 1)
    scatter_direct(1, 0)
    scatter_relay(1, 0)
    sum_quarter(0)
    scatter_near(0, 2)
    scatter_near(0, 1)
    sum_quarter(1)
    scatter_near(0, 0)
    for g in (2, 1, 0):
        scatter_near(1, g)
    y = scatter_end(0)

    d_prob = jnp.sum((gsel * y).reshape(CAP, KC, LC), axis=(1, 2), keepdims=True)
    d_prob = jnp.broadcast_to(d_prob, (CAP, KC, LC)).reshape(BR, LC)
    d_logit = d_prob * prob * (1.0 - prob)
    out_rows[0] = (prob * y).astype(BF16)
    dx = scatter_end(1)
    out_rows[1] = (dx + (d_logit * scale_in) * differ).astype(BF16)

    for h in range(2):
        for d in range(3):
            at = half((rep + 3 - d) % 4, h)
            arrived(ps.at[at, :], p_recv.at[d, h])
    out_pseudo[...] = ps[...]

    for c in pending:
        c.wait_send()


def finish(
    ids, rows, pseudo, params, momentum,
    out_mixed, out_grad, out_params, out_momentum,
    mixv, grdv, parv, momv, sem,
):
    def store(src, dst, i):
        c = pltpu.make_async_copy(src, dst, sem.at[i])
        c.start()
        return c


    rows8 = id_rows(ids)
    tri = one(iota((TOK, TOK), 0) >= iota((TOK, TOK), 1)).astype(BF16)
    eye = one(iota((TOK, TOK), 0) == iota((TOK, TOK), 1)).astype(BF16)
    slot = dot(tri, rows8, NT)[:, 0:1] - 1.0
    routed = dot(eye, rows8, NT)[:, 0:1]
    shape = (TOK, BR)
    mine = (slot == (iota(shape, 1) // KC).astype(F32)) & (routed > 0.5)
    spread = jnp.concatenate(
        [one(mine & (iota(shape, 1) % KC == k)).astype(BF16) for k in range(KC)], axis=0
    )
    stores = []
    for src, buf, dst in ((0, mixv, out_mixed), (1, grdv, out_grad)):
        placed = dot(spread, rows[src]).astype(BF16)
        for k in range(KC):
            buf[:, k * LC : (k + 1) * LC] = placed[k * TOK : (k + 1) * TOK]
        stores.append(store(buf, dst, 2 + src))
    shift = pseudo[...].astype(F32)
    mom = momentum_decay * momentum[...] + shift
    momv[...] = mom
    stores.append(store(momv, out_momentum, 0))
    parv[...] = params[...] - outer_rate * (shift + momentum_decay * mom)
    stores.append(store(parv, out_params, 1))
    for c in stores:
        c.wait()


def body(
    tokens,
    expert_ids,
    router_weight,
    expert_weights,
    outer_params,
    outer_momentum,
    inner_drift,
    frag_index,
    out_grad,
):
    vmem = pl.BlockSpec(memory_space=pltpu.VMEM)
    anyw = pl.BlockSpec(memory_space=pl.ANY)
    dma = pltpu.SemaphoreType.DMA
    scratch = [
        pltpu.VMEM((2, TOK), jnp.int32),
        pltpu.VMEM((1, EXPERTS, D), BF16),
        pltpu.VMEM((1, 1), jnp.int32),
        pltpu.VMEM((TOK, D), BF16),
        pltpu.VMEM((TOK, D), BF16),
        pltpu.VMEM((D, 4 * HID), BF16),
        pltpu.VMEM((D, 2 * HID), BF16),
        pltpu.VMEM((FR, HID), F32),
        pltpu.VMEM((256, 256), BF16),
        pltpu.VMEM((2, ROWS * KC, LC), BF16),
        pltpu.VMEM((ROWS, D), BF16),
        pltpu.VMEM((ROWS, D), BF16),
        pltpu.VMEM((2, KC, ROWS, LC), BF16),
        pltpu.VMEM((2, ROWS * KC, LC), BF16),
        pltpu.VMEM((2, 2, 4 * BR, LC), BF16),
        pltpu.VMEM((2, 2, 8 * BR, LC), BF16),
        pltpu.VMEM((2, 8, BR, LC), BF16),
        pltpu.VMEM((FR, HID), F32),
        pltpu.VMEM((FR, HID), BF16),
        pltpu.VMEM((FR, HID), BF16),
        pltpu.VMEM((FR, HID), BF16),
        pltpu.VMEM((3, 2, HR, HID), BF16),
        pltpu.VMEM((FR, HID), BF16),
        dma((9,)),
        dma((2, 8)),
        dma((2, 8)),
        dma((2, 3, 6)),
        dma((2, 4, 6)),
        dma((3,)),
        dma((3,)),
        dma((2, 2, 3)),
        dma((2, 2, 3)),
        dma((2, 2, 6)),
        dma((2, 2, 6)),
        dma((2, 8)),
        dma((2, 8)),
        dma,
        dma,
        dma((3, 2)),
        dma((3, 2)),
        dma((3, 2)),
        dma((3, 2)),
    ]
    ids = expert_ids.T
    rows, pseudo = pl.pallas_call(
        kernel,
        out_shape=(
            pltpu.VMEM((2, BR, LC), BF16),
            pltpu.VMEM((FR, HID), BF16),
        ),
        in_specs=[anyw] * 7,
        out_specs=(vmem, vmem),
        scratch_shapes=scratch,
        compiler_params=pltpu.CompilerParams(
            collective_id=0, has_side_effects=True, vmem_limit_bytes=56 * 1024 * 1024
        ),
        cost_estimate=pl.CostEstimate(
            flops=4_000_000_000, bytes_accessed=12_000_000, transcendentals=100_000
        ),
    )(
        tokens,
        ids,
        router_weight,
        expert_weights,
        inner_drift,
        frag_index.reshape(1, 1),
        out_grad,
    )
    return pl.pallas_call(
        finish,
        out_shape=(
            jax.ShapeDtypeStruct((TOK, D), BF16),
            jax.ShapeDtypeStruct((TOK, D), BF16),
            jax.ShapeDtypeStruct((FR, HID), F32),
            jax.ShapeDtypeStruct((FR, HID), F32),
        ),
        in_specs=[vmem] * 5,
        out_specs=(anyw, anyw, anyw, anyw),
        scratch_shapes=[
            pltpu.VMEM((TOK, D), BF16),
            pltpu.VMEM((TOK, D), BF16),
            pltpu.VMEM((FR, HID), F32),
            pltpu.VMEM((FR, HID), F32),
            dma((4,)),
        ],
        compiler_params=pltpu.CompilerParams(vmem_limit_bytes=16 * 1024 * 1024),
    )(ids, rows, pseudo, outer_params, outer_momentum)


def solution(mesh):
    in_specs = (
        P(("replica", "fsdp"), None),
        P(("replica", "fsdp"), None),
        P("replica", None, None),
        P("replica", None, None, "fsdp"),
        P(None, "fsdp"),
        P(None, "fsdp"),
        P("replica", None, "fsdp"),
        P(),
        P(("replica", "fsdp"), None),
    )
    out_specs = (
        P(("replica", "fsdp"), None),
        P(("replica", "fsdp"), None),
        P(None, "fsdp"),
        P(None, "fsdp"),
    )
    return jax.shard_map(body, mesh=mesh, in_specs=in_specs, out_specs=out_specs, check_vma=False)
```

time: 61.9 us -> 59.5 us (0.961)
  the two profiles are of different devices: /device:TPU:6 before, /device:TPU:1 now
where the time goes in v3:
time: 59.5 us; the launch traced here: 59.3 us
  Pallas kernels  58 us (97%)
  between operations  1.34 us (2%)
    pallas_call x1, Pallas kernels, body(): pl.pallas_call(kernel, out_shape=(pltpu.VMEM((2, BR, LC), BF16), pltpu.VM...  56 us
    pallas_call x1, Pallas kernels, body(): pl.pallas_call(finish, out_shape=(jax.ShapeDtypeStruct((TOK, D), BF16), j...  2.03 us

profile of v3, /device:TPU:1, one launch (start us, length us, event | category | flops | bytes accessed | tf_op | source)
XLA Modules:
  0.0 59.3 jit_solution(2872645463765200070)
XLA Ops:
  1.3 0.0 copy-start
  1.3 0.0 copy-start.1
  1.3 0.0 copy-start.2
  1.3 56.0 %shard_map.120 = (bf16[2,48,384]{2,1,0:T(8,128)(2,1)S(1)}, bf16[768,128]{1,0:T(8,128)(2,1)S(1)}) custom-call(bf16[64,6144]{1,0:T(8,128)(2,1)} %tokens.1, s32[2,64]{1,0:T(2,128)} %bitcast.3, bf16[1,8,6144]{2,1,0:T(8,128)(2,1)} %router_hbm.1, bf16[1,3,6144,128]{3,2,1,0:T(8,128)(2,1)} %weights.1, f32[1,768,128]{2,1,0:T(8,128)} %drift.1, ...), custom_call_target="tpu_custom_call" | custom-call | flops 4000000000 | bytes 12000000 | tf_op jit(solution)/shard_map/pallas_call | solution.py:576
  57.3 0.0 copy-done
  57.3 0.0 copy-done.1
  57.3 0.0 copy-done.2
  57.3 2.0 %shard_map.121 = (bf16[64,6144]{1,0:T(8,128)(2,1)}, bf16[64,6144]{1,0:T(8,128)(2,1)}, f32[768,128]{1,0:T(8,128)}, f32[768,128]{1,0:T(8,128)}) custom-call(s32[2,64]{1,0:T(2,128)S(1)} %bitcast.4, bf16[2,48,384]{2,1,0:T(8,128)(2,1)S(1)} %get-tuple-element.6.rows, bf16[768,128]{1,0:T(8,128)(2,1)S(1)} %get-tuple-element.7.pseudo, f32[768,128]{1,0:T(8,128)S(1)} %copy-done, ...), custom_call_target="tpu_custom_call" | custom-call | tf_op jit(solution)/shard_map/pallas_call | solution.py:600
Async XLA Ops:
  1.3 56.0 %copy-start = (f32[768,128]{1,0:T(8,128)S(1)}, f32[768,128]{1,0:T(8,128)}, u32[]{:S(2)}) copy-start(f32[768,128]{1,0:T(8,128)} %params.1) | copy-start | bytes 1179652
  1.3 56.0 %copy-start.1 = (f32[768,128]{1,0:T(8,128)S(1)}, f32[768,128]{1,0:T(8,128)}, u32[]{:S(2)}) copy-start(f32[768,128]{1,0:T(8,128)} %momentum.1) | copy-start | bytes 1179652
  1.3 56.0 %copy-start.2 = (s32[64,2]{0,1:T(2,128)S(1)}, s32[64,2]{0,1:T(2,128)}, u32[]{:S(2)}) copy-start(s32[64,2]{0,1:T(2,128)} %param.10) | copy-start | bytes 1540

commit v4 on v3

--- a/solution.py
+++ b/solution.py
@@ -243,36 +243,33 @@
         put(src, group(ag, i, 3, z, g), r_send.at[i, 0, j], r_recv.at[i, 3, j], up2)
         put(src, group(ag, i, 1, z, g), r_send.at[i, 1, j], r_recv.at[i, 1, j], dn2)
 
-    def near_to_ring(z, g):
-        for i in range(2):
-            for p in MEMBERS[g]:
-                arrived(piece(ag, i, 0, z, p), n_recv.at[i, z * 4 + p])
-            to_ring(i, z, g)
+    def near_to_ring(i, z, g):
+        for p in MEMBERS[g]:
+            arrived(piece(ag, i, 0, z, p), n_recv.at[i, z * 4 + p])
+        to_ring(i, z, g)
 
     def got_ring(i, slab, z, g):
         arrived(group(ag, i, slab, z, g), r_recv.at[i, slab, z * 3 + g])
 
-    def relay(z, g):
+    def relay(i, z, g):
         j = z * 3 + g
-        for i in range(2):
-            got_ring(i, 3, z, g)
-            if z == 0:
-                src = group(ag, i, 3, z, g)
-                put(src, group(ag, i, 2, z, g), r_send.at[i, 2, j], r_recv.at[i, 2, j], up2)
-            got_ring(i, 1, z, g)
-            if z == 1:
-                src = group(ag, i, 1, z, g)
-                put(src, group(ag, i, 2, z, g), r_send.at[i, 2, j], r_recv.at[i, 2, j], dn2)
-
-    def unfold(lo, hi):
+        got_ring(i, 3, z, g)
+        if z == 0:
+            src = group(ag, i, 3, z, g)
+            put(src, group(ag, i, 2, z, g), r_send.at[i, 2, j], r_recv.at[i, 2, j], up2)
+        got_ring(i, 1, z, g)
+        if z == 1:
+            src = group(ag, i, 1, z, g)
+            put(src, group(ag, i, 2, z, g), r_send.at[i, 2, j], r_recv.at[i, 2, j], dn2)
+
+    def unfold(i, dst, lo, hi):
         @pl.loop(lo, hi, unroll=True)
         def _(g):
             rows_at = pl.ds(pl.multiple_of(g * 16, 16), 16)
-            for i, dst in ((0, xv), (1, gv)):
-                v = ag[i, pl.ds(pl.multiple_of(g * 256, 256), 256), :]
-                r = dot(perm[...], v).astype(BF16)
-                for k in range(KC):
-                    dst[rows_at, k * LC : (k + 1) * LC] = r[16 * k : 16 * k + 16]
+            v = ag[i, pl.ds(pl.multiple_of(g * 256, 256), 256), :]
+            r = dot(perm[...], v).astype(BF16)
+            for k in range(KC):
+                dst[rows_at, k * LC : (k + 1) * LC] = r[16 * k : 16 * k + 16]
 
     to_ring(0, 0, 0)
     to_near(0)
@@ -292,15 +289,21 @@
     loads.append(load(drift.at[0], drfv, 5))
 
     order = [(0, 0), (1, 0), (0, 1), (1, 1), (0, 2), (1, 2)]
-    for z, g in order[1:]:
-        near_to_ring(z, g)
-    for z, g in order:
-        relay(z, g)
-    unfold(0, 3)
+    for j in range(1, 10):
+        if j < 6:
+            near_to_ring(0, *order[j])
+        if j > 4:
+            near_to_ring(1, *order[j - 4])
+    for j in range(10):
+        if j < 6:
+            relay(0, *order[j])
+        if j >= 4:
+            relay(1, *order[j - 4])
+    unfold(0, xv, 0, 3)
+    unfold(1, gv, 0, 3)
     for z, g in order:
         got_ring(0, 2, z, g)
-        got_ring(1, 2, z, g)
-    unfold(3, 6)
+    unfold(0, xv, 3, 6)
 
     for c in loads:
         c.wait()
@@ -312,6 +315,91 @@
     sigma = jax.nn.sigmoid(gate)
     active = gate * sigma
     hidden = (active * up).astype(BF16)
+    def back(i, rows_at, w, scale):
+        for k in range(KC):
+            part = dot(rows_at, w[k * LC : (k + 1) * LC, :], NT)
+            for c in range(LC // 128):
+                lanes = slice(c * 128, (c + 1) * 128)
+                yv[i, c, pl.ds(k, ROWS, stride=KC), :] = part[:, lanes] * scale
+
+    def refold(i, lo, hi):
+        at = pl.ds(lo * 256, (hi - lo) * 256)
+        for c in range(LC // 128):
+            rb[i, at, c * 128 : (c + 1) * 128] = yv[i, c, at, :].astype(BF16)
+
+    def transit(i, way, g):
+        at = pl.ds(GROUP[g][0] * BR, GROUP[g][1] * BR)
+        return t2.at[i, way, at, :]
+
+    def landing(i, way, z, g):
+        return d2.at[i, way, group_rows(0, z, g), :]
+
+    def send_transit(i, way, g, to):
+        put(
+            group(rb, i, 2, way, g), transit(i, way, g),
+            t2_send.at[i, way, g], t2_recv.at[i, way, g], to,
+        )
+
+    def send_landing(i, way, slab, z, g, to):
+        j = z * 3 + g
+        put(
+            group(rb, i, slab, z, g), landing(i, way, z, g),
+            d2_send.at[i, way, j], d2_recv.at[i, way, j], to,
+        )
+
+    def add_into(i, at, *others):
+        v = rb[i, at, :].astype(F32)
+        for other in others:
+            v = v + other[...].astype(F32)
+        rb[i, at, :] = v.astype(BF16)
+
+    def scatter_start(i):
+        refold(i, 3, 6)
+        for g in (2, 1, 0):
+            send_transit(i, 0, g, up2)
+            send_transit(i, 1, g, dn2)
+        refold(i, 0, 3)
+
+    def scatter_direct(i, g):
+        send_landing(i, 0, 1, 1, g, up2)
+        send_landing(i, 1, 3, 0, g, dn2)
+
+    def scatter_relay(i, g):
+        arrived(transit(i, 0, g), t2_recv.at[i, 0, g])
+        add_into(i, group_rows(1, 0, g), transit(i, 0, g))
+        send_landing(i, 0, 1, 0, g, up2)
+        arrived(transit(i, 1, g), t2_recv.at[i, 1, g])
+        add_into(i, group_rows(3, 1, g), transit(i, 1, g))
+        send_landing(i, 1, 3, 1, g, dn2)
+
+    def scatter_near(i, g):
+        for z in (1, 0):
+            for way in range(2):
+                arrived(landing(i, way, z, g), d2_recv.at[i, way, z * 3 + g])
+            add_into(i, group_rows(0, z, g), landing(i, 0, z, g), landing(i, 1, z, g))
+            for p in MEMBERS[g]:
+                if (z, p) != (0, 0):
+                    j = z * 4 + (4 - p) % 4
+                    put(
+                        piece(rb, i, 0, z, p), e1.at[i, j],
+                        e1_send.at[i, z * 4 + p], e1_recv.at[i, j], near[z, p],
+                    )
+
+    def scatter_end(i):
+        v = rb[i, 0:BR, :].astype(F32)
+        for z, p in far_last:
+            j = z * 4 + p
+            arrived(e1.at[i, j], e1_recv.at[i, j])
+            v = v + e1[i, j].astype(F32)
+        return v
+
+    back(0, hidden, wdn, scale_hid)
+    scatter_start(0)
+    for g in (2, 1, 0):
+        scatter_direct(0, g)
+    for z, g in order:
+        got_ring(1, 2, z, g)
+    unfold(1, gv, 3, 6)
     d_hidden = dot(gv[...], wdn[...]) * scale_hid
     d_gate = (d_hidden * up * (sigma + gate * sigma * (1.0 - sigma))).astype(BF16)
     d_up = (d_hidden * active).astype(BF16)
@@ -338,84 +426,7 @@
     put(fb, fs, f_send, f_recv, sib)
     fq[...] = partial[:, :HID] - drfv[...]
 
-    def back(i, rows_at, w, scale):
-        for k in range(KC):
-            part = dot(rows_at, w[k * LC : (k + 1) * LC, :], NT)
-            yv[i, k] = (part * scale).astype(BF16)
-
-    def refold(i, lo, hi):
-        @pl.loop(lo, hi, unroll=True)
-        def _(g):
-            v = yv[i, :, pl.ds(pl.multiple_of(g * 16, 16), 16), :].reshape(256, LC)
-            rb[i, pl.ds(pl.multiple_of(g * 256, 256), 256), :] = dot(perm[...], v).astype(BF16)
-
-    def transit(i, way, g):
-        at = pl.ds(GROUP[g][0] * BR, GROUP[g][1] * BR)
-        return t2.at[i, way, at, :]
-
-    def landing(i, way, z, g):
-        return d2.at[i, way, group_rows(0, z, g), :]
-
-    def send_transit(i, way, g, to):
-        put(
-            group(rb, i, 2, way, g), transit(i, way, g),
-            t2_send.at[i, way, g], t2_recv.at[i, way, g], to,
-        )
-
-    def send_landing(i, way, slab, z, g, to):
-        j = z * 3 + g
-        put(
-            group(rb, i, slab, z, g), landing(i, way, z, g),
-            d2_send.at[i, way, j], d2_recv.at[i, way, j], to,
-        )
-
-    def add_into(i, at, *others):
-        v = rb[i, at, :].astype(F32)
-        for other in others:
-            v = v + other[...].astype(F32)
-        rb[i, at, :] = v.astype(BF16)
-
-    def scatter_start(i):
-        refold(i, 3, 6)
-        for g in (2, 1, 0):
-            send_transit(i, 0, g, up2)
-            send_transit(i, 1, g, dn2)
-        refold(i, 0, 3)
-
-    def scatter_direct(i, g):
-        send_landing(i, 0, 1, 1, g, up2)
-        send_landing(i, 1, 3, 0, g, dn2)
-
-    def scatter_relay(i, g):
-        arrived(transit(i, 0, g), t2_recv.at[i, 0, g])
-        add_into(i, group_rows(1, 0, g), transit(i, 0, g))
-        send_landing(i, 0, 1, 0, g, up2)
-        arrived(transit(i, 1, g), t2_recv.at[i, 1, g])
-        add_into(i, group_rows(3, 1, g), transit(i, 1, g))
-        send_landing(i, 1, 3, 1, g, dn2)
-
-    def scatter_near(i, g):
-        for z in (1, 0):
-            for way in range(2):
-                arrived(landing(i, way, z, g), d2_recv.at[i, way, z * 3 + g])
-            add_into(i, group_rows(0, z, g), landing(i, 0, z, g), landing(i, 1, z, g))
-            for p in MEMBERS[g]:
-                if (z, p) != (0, 0):
-                    j = z * 4 + (4 - p) % 4
-                    put(
-                        piece(rb, i, 0, z, p), e1.at[i, j],
-                        e1_send.at[i, z * 4 + p], e1_recv.at[i, j], near[z, p],
-                    )
-
-    def scatter_end(i):
-        v = rb[i, 0:BR, :].astype(F32)
-        for z, p in far_last:
-            j = z * 4 + p
-            arrived(e1.at[i, j], e1_recv.at[i, j])
-            v = v + e1[i, j].astype(F32)
-        return v
-
-    back(0, hidden, wdn, scale_hid)
+    back(1, d_gu, wgu, scale_in)
     arrived(fs, f_recv)
     fq[...] = fq[...] + fs[...].astype(F32)
     fh[...] = fq[...].astype(BF16)
@@ -438,26 +449,24 @@
         for d in (1, 0, 2):
             put(ps.at[own, :], ps.at[own, :], p_send.at[d, h], p_recv.at[d, h], reps[d])
 
-    scatter_start(0)
-    for g in (2, 1, 0):
-        scatter_direct(0, g)
-    back(1, d_gu, wgu, scale_in)
     scatter_start(1)
-    for g in (2, 1, 0):
-        scatter_relay(0, g)
+    scatter_relay(0, 2)
+    scatter_relay(0, 1)
+    scatter_relay(0, 0)
     scatter_direct(1, 2)
+    scatter_direct(1, 1)
     scatter_relay(1, 2)
-    scatter_direct(1, 1)
+    scatter_near(0, 2)
+    scatter_direct(1, 0)
     scatter_relay(1, 1)
-    scatter_direct(1, 0)
+    scatter_near(0, 1)
     scatter_relay(1, 0)
+    scatter_near(0, 0)
     sum_quarter(0)
-    scatter_near(0, 2)
-    scatter_near(0, 1)
     sum_quarter(1)
-    scatter_near(0, 0)
-    for g in (2, 1, 0):
-        scatter_near(1, g)
+    scatter_near(1, 2)
+    scatter_near(1, 1)
+    scatter_near(1, 0)
     y = scatter_end(0)
 
     d_prob = jnp.sum((gsel * y).reshape(CAP, KC, LC), axis=(1, 2), keepdims=True)
@@ -541,7 +550,7 @@
         pltpu.VMEM((2, ROWS * KC, LC), BF16),
         pltpu.VMEM((ROWS, D), BF16),
         pltpu.VMEM((ROWS, D), BF16),
-        pltpu.VMEM((2, KC, ROWS, LC), BF16),
+        pltpu.VMEM((2, LC // 128, ROWS * KC, 128), F32),
         pltpu.VMEM((2, ROWS * KC, LC), BF16),
         pltpu.VMEM((2, 2, 4 * BR, LC), BF16),
         pltpu.VMEM((2, 2, 8 * BR, LC), BF16),

time: 59.5 us -> 53.9 us (0.906)
  the two profiles are of different devices: /device:TPU:1 before, /device:TPU:6 now
where the time goes in v4:
time: 53.9 us; the launch traced here: 53.7 us
  Pallas kernels  52.3 us (97%)
  between operations  1.34 us (2%)
    pallas_call x1, Pallas kernels, body(): pl.pallas_call(kernel, out_shape=(pltpu.VMEM((2, BR, LC), BF16), pltpu.VM...  50.3 us
    pallas_call x1, Pallas kernels, body(): pl.pallas_call(finish, out_shape=(jax.ShapeDtypeStruct((TOK, D), BF16), j...  2.03 us

profile of v4, /device:TPU:6, one launch (start us, length us, event | category | flops | bytes accessed | tf_op | source)
XLA Modules:
  0.0 53.7 jit_solution(17381368475178644518)
XLA Ops:
  1.3 0.0 copy-start
  1.3 0.0 copy-start.1
  1.3 0.0 copy-start.2
  1.3 50.3 %shard_map.120 = (bf16[2,48,384]{2,1,0:T(8,128)(2,1)S(1)}, bf16[768,128]{1,0:T(8,128)(2,1)S(1)}) custom-call(bf16[64,6144]{1,0:T(8,128)(2,1)} %tokens.1, s32[2,64]{1,0:T(2,128)} %bitcast.3, bf16[1,8,6144]{2,1,0:T(8,128)(2,1)} %router_hbm.1, bf16[1,3,6144,128]{3,2,1,0:T(8,128)(2,1)} %weights.1, f32[1,768,128]{2,1,0:T(8,128)} %drift.1, ...), custom_call_target="tpu_custom_call" | custom-call | flops 4000000000 | bytes 12000000 | tf_op jit(solution)/shard_map/pallas_call | solution.py:585
  51.6 0.0 copy-done
  51.6 0.0 copy-done.1
  51.6 0.0 copy-done.2
  51.6 2.0 %shard_map.121 = (bf16[64,6144]{1,0:T(8,128)(2,1)}, bf16[64,6144]{1,0:T(8,128)(2,1)}, f32[768,128]{1,0:T(8,128)}, f32[768,128]{1,0:T(8,128)}) custom-call(s32[2,64]{1,0:T(2,128)S(1)} %bitcast.4, bf16[2,48,384]{2,1,0:T(8,128)(2,1)S(1)} %get-tuple-element.6.rows, bf16[768,128]{1,0:T(8,128)(2,1)S(1)} %get-tuple-element.7.pseudo, f32[768,128]{1,0:T(8,128)S(1)} %copy-done, ...), custom_call_target="tpu_custom_call" | custom-call | tf_op jit(solution)/shard_map/pallas_call | solution.py:609
Async XLA Ops:
  1.3 50.3 %copy-start = (f32[768,128]{1,0:T(8,128)S(1)}, f32[768,128]{1,0:T(8,128)}, u32[]{:S(2)}) copy-start(f32[768,128]{1,0:T(8,128)} %params.1) | copy-start | bytes 1179652
  1.3 50.3 %copy-start.1 = (f32[768,128]{1,0:T(8,128)S(1)}, f32[768,128]{1,0:T(8,128)}, u32[]{:S(2)}) copy-start(f32[768,128]{1,0:T(8,128)} %momentum.1) | copy-start | bytes 1179652
  1.3 50.3 %copy-start.2 = (s32[64,2]{0,1:T(2,128)S(1)}, s32[64,2]{0,1:T(2,128)}, u32[]{:S(2)}) copy-start(s32[64,2]{0,1:T(2,128)} %param.10) | copy-start | bytes 1540

commit v5 on v4

--- a/solution.py
+++ b/solution.py
@@ -188,6 +188,72 @@
         & (iota(sshape, 0) % KC == iota(sshape, 1) // TOK)
     )
     select = one(smask).astype(BF16)
+    def fold(ref):
+        stacked = jnp.concatenate([ref[:, k * LC : (k + 1) * LC] for k in range(KC)], axis=0)
+        return dot(select, stacked)
+
+    load_tok.wait()
+    xsel = fold(tokv)
+    ag[0, 0:BR, :] = xsel.astype(BF16)
+
+    pl.semaphore_wait(barrier, len(peers))
+
+    def piece(ref, i, slab, z, p):
+        return ref.at[i, pl.ds(row(slab, z, p), BR), :]
+
+    def group(ref, i, slab, z, g):
+        return ref.at[i, group_rows(slab, z, g), :]
+
+    def put(src, dst, ssem, rsem, to):
+        pending.append(send(src, dst, ssem, rsem, to))
+
+    far_last = [(1, 0), (0, 1), (0, 3), (1, 1), (1, 3), (0, 2), (1, 2)]
+
+    def to_near(i):
+        for z, p in far_last:
+            q = (4 - p) % 4
+            put(
+                piece(ag, i, 0, 0, 0), piece(ag, i, 0, z, q),
+                n_send.at[i, z * 4 + p], n_recv.at[i, z * 4 + q], near[z, p],
+            )
+
+    def to_ring(i, z, g):
+        j = z * 3 + g
+        src = group(ag, i, 0, z, g)
+        put(src, group(ag, i, 3, z, g), r_send.at[i, 0, j], r_recv.at[i, 3, j], up2)
+        put(src, group(ag, i, 1, z, g), r_send.at[i, 1, j], r_recv.at[i, 1, j], dn2)
+
+    def near_to_ring(i, z, g):
+        for p in MEMBERS[g]:
+            arrived(piece(ag, i, 0, z, p), n_recv.at[i, z * 4 + p])
+        to_ring(i, z, g)
+
+    def got_ring(i, slab, z, g):
+        arrived(group(ag, i, slab, z, g), r_recv.at[i, slab, z * 3 + g])
+
+    def relay(i, z, g):
+        j = z * 3 + g
+        got_ring(i, 3, z, g)
+        if z == 0:
+            src = group(ag, i, 3, z, g)
+            put(src, group(ag, i, 2, z, g), r_send.at[i, 2, j], r_recv.at[i, 2, j], up2)
+        got_ring(i, 1, z, g)
+        if z == 1:
+            src = group(ag, i, 1, z, g)
+            put(src, group(ag, i, 2, z, g), r_send.at[i, 2, j], r_recv.at[i, 2, j], dn2)
+
+    def unfold(i, dst, lo, hi):
+        @pl.loop(lo, hi, unroll=True)
+        def _(g):
+            rows_at = pl.ds(pl.multiple_of(g * 16, 16), 16)
+            v = ag[i, pl.ds(pl.multiple_of(g * 256, 256), 256), :]
+            r = dot(perm[...], v).astype(BF16)
+            for k in range(KC):
+                dst[rows_at, k * LC : (k + 1) * LC] = r[16 * k : 16 * k + 16]
+
+    to_ring(0, 0, 0)
+    to_near(0)
+
     other48 = jnp.sum(jnp.where(smask, tiled[1:2], 0.0), axis=1, keepdims=True)
     dshape = (BR, KC * EXPERTS)
     expert = iota(dshape, 1) % EXPERTS
@@ -207,72 +273,6 @@
         (iota(pshape, 0) // 16 == iota(pshape, 1) % 16)
         & (iota(pshape, 0) % 16 == iota(pshape, 1) // 16)
     ).astype(BF16)
-
-    def fold(ref):
-        stacked = jnp.concatenate([ref[:, k * LC : (k + 1) * LC] for k in range(KC)], axis=0)
-        return dot(select, stacked)
-
-    load_tok.wait()
-    xsel = fold(tokv)
-    ag[0, 0:BR, :] = xsel.astype(BF16)
-
-    pl.semaphore_wait(barrier, len(peers))
-
-    def piece(ref, i, slab, z, p):
-        return ref.at[i, pl.ds(row(slab, z, p), BR), :]
-
-    def group(ref, i, slab, z, g):
-        return ref.at[i, group_rows(slab, z, g), :]
-
-    def put(src, dst, ssem, rsem, to):
-        pending.append(send(src, dst, ssem, rsem, to))
-
-    far_last = [(1, 0), (0, 1), (0, 3), (1, 1), (1, 3), (0, 2), (1, 2)]
-
-    def to_near(i):
-        for z, p in far_last:
-            q = (4 - p) % 4
-            put(
-                piece(ag, i, 0, 0, 0), piece(ag, i, 0, z, q),
-                n_send.at[i, z * 4 + p], n_recv.at[i, z * 4 + q], near[z, p],
-            )
-
-    def to_ring(i, z, g):
-        j = z * 3 + g
-        src = group(ag, i, 0, z, g)
-        put(src, group(ag, i, 3, z, g), r_send.at[i, 0, j], r_recv.at[i, 3, j], up2)
-        put(src, group(ag, i, 1, z, g), r_send.at[i, 1, j], r_recv.at[i, 1, j], dn2)
-
-    def near_to_ring(i, z, g):
-        for p in MEMBERS[g]:
-            arrived(piece(ag, i, 0, z, p), n_recv.at[i, z * 4 + p])
-        to_ring(i, z, g)
-
-    def got_ring(i, slab, z, g):
-        arrived(group(ag, i, slab, z, g), r_recv.at[i, slab, z * 3 + g])
-
-    def relay(i, z, g):
-        j = z * 3 + g
-        got_ring(i, 3, z, g)
-        if z == 0:
-            src = group(ag, i, 3, z, g)
-            put(src, group(ag, i, 2, z, g), r_send.at[i, 2, j], r_recv.at[i, 2, j], up2)
-        got_ring(i, 1, z, g)
-        if z == 1:
-            src = group(ag, i, 1, z, g)
-            put(src, group(ag, i, 2, z, g), r_send.at[i, 2, j], r_recv.at[i, 2, j], dn2)
-
-    def unfold(i, dst, lo, hi):
-        @pl.loop(lo, hi, unroll=True)
-        def _(g):
-            rows_at = pl.ds(pl.multiple_of(g * 16, 16), 16)
-            v = ag[i, pl.ds(pl.multiple_of(g * 256, 256), 256), :]
-            r = dot(perm[...], v).astype(BF16)
-            for k in range(KC):
-                dst[rows_at, k * LC : (k + 1) * LC] = r[16 * k : 16 * k + 16]
-
-    to_ring(0, 0, 0)
-    to_near(0)
     logit = jnp.sum((xsel * differ).reshape(CAP, KC, LC), axis=(1, 2), keepdims=True)
     prob = jax.nn.sigmoid(jnp.broadcast_to(logit * scale_in, (CAP, KC, LC)).reshape(BR, LC))
     load_grd.wait()
@@ -427,6 +427,10 @@
     fq[...] = partial[:, :HID] - drfv[...]
 
     back(1, d_gu, wgu, scale_in)
+    scatter_start(1)
+    scatter_relay(0, 2)
+    scatter_relay(0, 1)
+    scatter_relay(0, 0)
     arrived(fs, f_recv)
     fq[...] = fq[...] + fs[...].astype(F32)
     fh[...] = fq[...].astype(BF16)
@@ -449,10 +453,6 @@
         for d in (1, 0, 2):
             put(ps.at[own, :], ps.at[own, :], p_send.at[d, h], p_recv.at[d, h], reps[d])
 
-    scatter_start(1)
-    scatter_relay(0, 2)
-    scatter_relay(0, 1)
-    scatter_relay(0, 0)
     scatter_direct(1, 2)
     scatter_direct(1, 1)
     scatter_relay(1, 2)

time: 53.9 us -> 54 us (level)
  no operation moved by 1% of the time
where the time goes in v5:
time: 54 us; the launch traced here: 53.9 us
  Pallas kernels  52.5 us (97%)
  between operations  1.34 us (2%)
    pallas_call x1, Pallas kernels, body(): pl.pallas_call(kernel, out_shape=(pltpu.VMEM((2, BR, LC), BF16), pltpu.VM...  50.5 us
    pallas_call x1, Pallas kernels, body(): pl.pallas_call(finish, out_shape=(jax.ShapeDtypeStruct((TOK, D), BF16), j...  2.03 us

profile of v5, /device:TPU:6, one launch (start us, length us, event | category | flops | bytes accessed | tf_op | source)
XLA Modules:
  0.0 53.9 jit_solution(3590145953593149848)
XLA Ops:
  1.3 0.0 copy-start
  1.3 0.0 copy-start.1
  1.3 0.0 copy-start.2
  1.3 50.5 %shard_map.120 = (bf16[2,48,384]{2,1,0:T(8,128)(2,1)S(1)}, bf16[768,128]{1,0:T(8,128)(2,1)S(1)}) custom-call(bf16[64,6144]{1,0:T(8,128)(2,1)} %tokens.1, s32[2,64]{1,0:T(2,128)} %bitcast.3, bf16[1,8,6144]{2,1,0:T(8,128)(2,1)} %router_hbm.1, bf16[1,3,6144,128]{3,2,1,0:T(8,128)(2,1)} %weights.1, f32[1,768,128]{2,1,0:T(8,128)} %drift.1, ...), custom_call_target="tpu_custom_call" | custom-call | flops 4000000000 | bytes 12000000 | tf_op jit(solution)/shard_map/pallas_call | solution.py:585
  51.8 0.0 copy-done
  51.8 0.0 copy-done.1
  51.9 0.0 copy-done.2
  51.9 2.0 %shard_map.121 = (bf16[64,6144]{1,0:T(8,128)(2,1)}, bf16[64,6144]{1,0:T(8,128)(2,1)}, f32[768,128]{1,0:T(8,128)}, f32[768,128]{1,0:T(8,128)}) custom-call(s32[2,64]{1,0:T(2,128)S(1)} %bitcast.4, bf16[2,48,384]{2,1,0:T(8,128)(2,1)S(1)} %get-tuple-element.6.rows, bf16[768,128]{1,0:T(8,128)(2,1)S(1)} %get-tuple-element.7.pseudo, f32[768,128]{1,0:T(8,128)S(1)} %copy-done, ...), custom_call_target="tpu_custom_call" | custom-call | tf_op jit(solution)/shard_map/pallas_call | solution.py:609
Async XLA Ops:
  1.3 50.6 %copy-start = (f32[768,128]{1,0:T(8,128)S(1)}, f32[768,128]{1,0:T(8,128)}, u32[]{:S(2)}) copy-start(f32[768,128]{1,0:T(8,128)} %params.1) | copy-start | bytes 1179652
  1.3 50.6 %copy-start.1 = (f32[768,128]{1,0:T(8,128)S(1)}, f32[768,128]{1,0:T(8,128)}, u32[]{:S(2)}) copy-start(f32[768,128]{1,0:T(8,128)} %momentum.1) | copy-start | bytes 1179652
  1.3 50.6 %copy-start.2 = (s32[64,2]{0,1:T(2,128)S(1)}, s32[64,2]{0,1:T(2,128)}, u32[]{:S(2)}) copy-start(s32[64,2]{0,1:T(2,128)} %param.10) | copy-start | bytes 1540
